TPU v7x, 32 devices: a whole 2x2x4 slice. The times are simulated.
32 devices in a mesh: seq: 2 (over y), ctx: 4 (over x, core), fsdp: 4 (over z).
Axes of the slice: x: 2, y: 2, z: 4, core: 2. Of those that a mesh axis runs over, the one named last changes fastest.
Arguments:
- tokens: bfloat16 [8, 1024, 2048], P(('seq', 'fsdp'), 'ctx'), may hold values from -6 to 6
- block_place: int32 [8, 8], P(('seq', 'fsdp')), may hold values from 0 to 7, each once within a row
- w_qkv: bfloat16 [2048, 6144], P('fsdp'), may hold values from -0.125 to 0.125
- b_qkv: bfloat16 [6144], P('fsdp'), may hold values from -2 to 2
- w_o_t: bfloat16 [2048, 2048], P('fsdp'), may hold values from -0.5 to 0.5
- b_o: bfloat16 [2048], P('fsdp'), may hold values from -2 to 2
- w_up: bfloat16 [2048, 8192], P('fsdp'), may hold values from -0.125 to 0.125
- b_up: bfloat16 [8192], P('fsdp'), may hold values from -2 to 2
- w_down_t: bfloat16 [2048, 8192], P('fsdp'), may hold values from -0.0625 to 0.0625
- b_down: bfloat16 [2048], P('fsdp'), may hold values from -2 to 2
- norm1_gain: bfloat16 [2048], P('fsdp'), may hold values from 0.5 to 1.5
- norm1_shift: bfloat16 [2048], P('fsdp'), may hold values from -2 to 2
- norm2_gain: bfloat16 [2048], P('fsdp'), may hold values from 0.5 to 1.5
- norm2_shift: bfloat16 [2048], P('fsdp'), may hold values from -2 to 2
- cotangent: bfloat16 [8, 1024, 2048], P(('seq', 'fsdp'), 'ctx'), may hold values from -6 to 6
Outputs:
- output: bfloat16 [8, 1024, 2048], P(('seq', 'fsdp'), 'ctx')
- input_grad: bfloat16 [8, 1024, 2048], P(('seq', 'fsdp'), 'ctx')
- grad_w_qkv: float32 [2048, 6144], P('fsdp')
- grad_b_qkv: float32 [6144], P('fsdp')
- grad_w_o_t: float32 [2048, 2048], P('fsdp')
- grad_b_o: float32 [2048], P('fsdp')
- grad_w_up: float32 [2048, 8192], P('fsdp')
- grad_b_up: float32 [8192], P('fsdp')
- grad_w_down_t: float32 [2048, 8192], P('fsdp')
- grad_b_down: float32 [2048], P('fsdp')
- grad_norm1_gain: float32 [2048], P('fsdp')
- grad_norm1_shift: float32 [2048], P('fsdp')
- grad_norm2_gain: float32 [2048], P('fsdp')
- grad_norm2_shift: float32 [2048], P('fsdp')
Inputs may be any that keep to these rules, and one draw needn't show every extreme that they name: Each row of block_place lists every block place of the sequence once.
All inputs are finite; a program needn't handle non-finite values.
Results may differ from a plain program's by a relative error of at most 0.015.
Values may be sent and summed in bfloat16 or wider, within the bound.
A program may use at most 704 MiB of HBM per device.

v0:
```python
import math

import jax
import jax.numpy as jnp
from jax import lax
from jax.sharding import PartitionSpec as P

D = 2048
HEADS = 8
HEAD = 256
ROT = 64
BLK = 128


eps = 1e-05


def norm_rows(values, gain_row, offset):
    middle = jnp.mean(values, -1, keepdims=True)
    centred = values - middle
    spread = jnp.mean(centred * centred, -1, keepdims=True)
    return centred * lax.rsqrt(spread + eps) * gain_row + offset


def angles(positions):
    freqs = 10000.0 ** (-(jnp.arange(ROT // 2, dtype=jnp.float32) * 2.0 / ROT))
    turned = positions.astype(jnp.float32)[:, None] * freqs[None, :]
    turned = jnp.concatenate([turned, turned], -1)
    return (jnp.cos(turned), jnp.sin(turned))


def rotate(values, cosine, sine):
    half = ROT // 2
    rotary = values[..., :ROT]
    swapped = jnp.concatenate([-rotary[..., half:], rotary[..., :half]], -1)
    moved = rotary * cosine[:, None, :] + swapped * sine[:, None, :]
    return jnp.concatenate([moved, values[..., ROT:]], -1)


def times_last(left, right):
    return lax.dot_general(
        left, right, (((1,), (1,)), ((), ())), preferred_element_type=jnp.float32
    )


def times_first(left, right):
    return lax.dot_general(
        left, right, (((0,), (0,)), ((), ())), preferred_element_type=jnp.float32
    )


def body(
    tokens,
    block_place,
    w_qkv,
    b_qkv,
    w_o_t,
    b_o,
    w_up,
    b_up,
    w_down_t,
    b_down,
    norm1_gain,
    norm1_shift,
    norm2_gain,
    norm2_shift,
    cotangent,
):
    low_type = jnp.bfloat16
    wide_type = jnp.float32
    inputs = tokens[0].astype(wide_type)
    tok_rows = inputs.shape[0]
    gathered = (
        lax.all_gather(b_qkv, "fsdp", axis=0, tiled=True),
        lax.all_gather(b_o, "fsdp", axis=0, tiled=True),
        lax.all_gather(b_up, "fsdp", axis=0, tiled=True),
        lax.all_gather(b_down, "fsdp", axis=0, tiled=True),
        lax.all_gather(norm1_gain, "fsdp", axis=0, tiled=True),
        lax.all_gather(norm1_shift, "fsdp", axis=0, tiled=True),
        lax.all_gather(norm2_gain, "fsdp", axis=0, tiled=True),
        lax.all_gather(norm2_shift, "fsdp", axis=0, tiled=True),
    )
    bias_qkv, bias_out, bias_up, bias_down, gain_one, shift_one, gain_two, shift_two = [
        g.astype(wide_type) for g in gathered
    ]
    normed_one, pull_one = jax.vjp(norm_rows, inputs, gain_one, shift_one)
    normed_two, pull_two = jax.vjp(norm_rows, inputs, gain_two, shift_two)
    low_one = normed_one.astype(low_type)
    low_two = normed_two.astype(low_type)
    pieces = (
        lax.all_gather(w_qkv, "fsdp", axis=0, tiled=True),
        lax.all_gather(w_up, "fsdp", axis=0, tiled=True),
    )
    projected = jnp.dot(low_one, pieces[0], preferred_element_type=wide_type)
    hidden = jnp.dot(low_two, pieces[1], preferred_element_type=wide_type)
    projected = projected + bias_qkv
    hidden = hidden + bias_up
    places = block_place[0]
    cycle_index = lax.axis_index("ctx")
    own_blocks = lax.dynamic_slice_in_dim(places, 2 * cycle_index, 2, 0)
    offsets = jnp.arange(BLK, dtype=jnp.int32)
    query_pos = (own_blocks[:, None] * BLK + offsets[None, :]).reshape(-1)
    key_pos = (places[:, None] * BLK + offsets[None, :]).reshape(-1)
    cosine, sine = angles(query_pos)

    def turn_heads(values):
        return rotate(values.reshape(tok_rows, HEADS, HEAD), cosine, sine)

    query_rot, query_pull = jax.vjp(turn_heads, projected[:, :D])
    key_rot, key_pull = jax.vjp(turn_heads, projected[:, D : 2 * D])
    queries = jnp.transpose(query_rot, (1, 0, 2)).astype(low_type)
    own_keys = jnp.transpose(key_rot, (1, 0, 2)).astype(low_type)
    own_values = jnp.transpose(
        projected[:, 2 * D :].reshape(tok_rows, HEADS, HEAD), (1, 0, 2)
    ).astype(low_type)
    keys_heads, values_heads = (
        lax.all_gather(own_keys, "ctx", axis=1, tiled=True),
        lax.all_gather(own_values, "ctx", axis=1, tiled=True),
    )
    scaling = 1.0 / math.sqrt(HEAD)
    allowed = query_pos[:, None] >= key_pos[None, :]

    def head_forward(item):
        query_part, key_part, value_part = item
        scores = jnp.where(allowed, times_last(query_part, key_part) * scaling, -1e30)
        top = jnp.max(scores, -1, keepdims=True)
        expo = jnp.exp(scores - top)
        total = jnp.sum(expo, -1, keepdims=True)
        weights_low = (expo / total).astype(low_type)
        return (
            jnp.dot(weights_low, value_part, preferred_element_type=wide_type),
            top[:, 0],
            total[:, 0],
        )

    attended_h, row_top, row_total = lax.map(head_forward, (queries, keys_heads, values_heads))
    attended_low = jnp.transpose(attended_h, (1, 0, 2)).reshape(tok_rows, D).astype(low_type)
    gelu_out, gelu_pull = jax.vjp(lambda values: jax.nn.gelu(values, approximate=False), hidden)
    gelu_low = gelu_out.astype(low_type)
    grad_low = cotangent[0]
    grad_wide = grad_low.astype(wide_type)
    pieces = (
        lax.all_gather(w_o_t, "fsdp", axis=0, tiled=True),
        lax.all_gather(w_down_t, "fsdp", axis=0, tiled=True),
    )
    partial_value = times_last(attended_low, pieces[0]) + times_last(gelu_low, pieces[1])
    d_attended = jnp.dot(grad_low, pieces[0], preferred_element_type=wide_type)
    d_gelu = jnp.dot(grad_low, pieces[1], preferred_element_type=wide_type)
    output = (inputs + partial_value + bias_out + bias_down).astype(low_type)[None]
    d_attended_low = d_attended.astype(low_type)
    d_hidden_low = gelu_pull(d_gelu)[0].astype(low_type)
    heads_grad = jnp.transpose(d_attended_low.reshape(tok_rows, HEADS, HEAD), (1, 0, 2))

    def query_side(query_part, key_part, value_part, grad_part, top, total):
        scores = jnp.where(allowed, times_last(query_part, key_part) * scaling, -1e30)
        weights = jnp.exp(scores - top[:, None]) / total[:, None]
        d_weights = times_last(grad_part, value_part)
        inner = jnp.sum(weights * d_weights, -1)
        d_scores_low = jnp.where(allowed, weights * (d_weights - inner[:, None]), 0.0).astype(
            low_type
        )
        d_query = jnp.dot(d_scores_low, key_part, preferred_element_type=wide_type) * scaling
        return (d_query, inner, d_scores_low, weights.astype(low_type))

    def head_back_kept(item):
        d_query, inner, d_scores_low, weights_low = query_side(*item)
        return (d_query, d_scores_low, weights_low)

    d_queries_h, d_scores_all, weights_all = lax.map(
        head_back_kept, (queries, keys_heads, values_heads, heads_grad, row_top, row_total)
    )
    d_keys = (
        jnp.einsum("hts,htd->shd", d_scores_all, queries, preferred_element_type=wide_type)
        * scaling
    )
    d_values = jnp.einsum("hts,htd->shd", weights_all, heads_grad, preferred_element_type=wide_type)
    key_grads = lax.psum_scatter(
        jnp.concatenate(
            [
                d_keys.reshape(tok_rows * lax.axis_size("ctx"), D),
                d_values.reshape(tok_rows * lax.axis_size("ctx"), D),
            ],
            1,
        ).astype(jnp.bfloat16),
        "ctx",
        scatter_dimension=0,
        tiled=True,
    ).astype(jnp.float32)
    d_keys_own = key_grads[:, :D]
    d_values_own = key_grads[:, D:]
    d_queries = jnp.transpose(d_queries_h, (1, 0, 2))
    d_query_pre = query_pull(d_queries)[0]
    d_key_pre = key_pull(d_keys_own.reshape(tok_rows, HEADS, HEAD))[0]
    d_projected_low = jnp.concatenate([d_query_pre, d_key_pre, d_values_own], 1).astype(low_type)
    pieces = (
        lax.all_gather(w_qkv, "fsdp", axis=0, tiled=True),
        lax.all_gather(w_up, "fsdp", axis=0, tiled=True),
    )
    part_one = times_last(d_projected_low, pieces[0])
    part_two = times_last(d_hidden_low, pieces[1])
    d_in_one, d_gain_one, d_shift_one = pull_one(part_one)
    d_in_two, d_gain_two, d_shift_two = pull_two(part_two)
    input_grad = (grad_wide + d_in_one + d_in_two).astype(low_type)[None]
    small_sums = lax.psum(
        (
            jnp.sum(d_projected_low, 0, dtype=wide_type),
            jnp.sum(grad_wide, 0),
            jnp.sum(d_hidden_low, 0, dtype=wide_type),
            d_gain_one,
            d_shift_one,
            d_gain_two,
            d_shift_two,
        ),
        ("seq", "ctx", "fsdp"),
    )
    shards = lax.axis_size("fsdp")
    fsdp_index = lax.axis_index("fsdp")

    def own_share(values):
        width = values.shape[0] // shards
        return lax.dynamic_slice_in_dim(values, fsdp_index * width, width, 0)

    in_part = lax.psum_scatter(
        jnp.concatenate(
            [times_first(low_one, d_projected_low), times_first(low_two, d_hidden_low)], 1
        ).astype(jnp.bfloat16),
        "fsdp",
        scatter_dimension=0,
        tiled=True,
    ).astype(jnp.float32)
    out_part = lax.psum_scatter(
        jnp.concatenate(
            [times_first(grad_low, attended_low), times_first(grad_low, gelu_low)], 1
        ).astype(jnp.bfloat16),
        "fsdp",
        scatter_dimension=0,
        tiled=True,
    ).astype(jnp.float32)
    in_part, out_part = (
        lax.psum(in_part.astype(jnp.bfloat16), ("seq", "ctx")).astype(jnp.float32),
        lax.psum(out_part.astype(jnp.bfloat16), ("seq", "ctx")).astype(jnp.float32),
    )
    grad_w_qkv = in_part[:, : 3 * D]
    grad_w_up = in_part[:, 3 * D :]
    grad_w_o_t = out_part[:, :D]
    grad_w_down_t = out_part[:, D:]
    grad_bias_out = own_share(small_sums[1])
    return (
        output,
        input_grad,
        grad_w_qkv,
        own_share(small_sums[0]),
        grad_w_o_t,
        grad_bias_out,
        grad_w_up,
        own_share(small_sums[2]),
        grad_w_down_t,
        grad_bias_out,
        own_share(small_sums[3]),
        own_share(small_sums[4]),
        own_share(small_sums[5]),
        own_share(small_sums[6]),
    )


def solution(mesh):
    in_specs = (
        P(("seq", "fsdp"), "ctx", None),
        P(("seq", "fsdp"), None),
        P("fsdp", None),
        P("fsdp"),
        P("fsdp", None),
        P("fsdp"),
        P("fsdp", None),
        P("fsdp"),
        P("fsdp", None),
        P("fsdp"),
        P("fsdp"),
        P("fsdp"),
        P("fsdp"),
        P("fsdp"),
        P(("seq", "fsdp"), "ctx", None),
    )
    out_specs = (
        P(("seq", "fsdp"), "ctx", None),
        P(("seq", "fsdp"), "ctx", None),
        P("fsdp", None),
        P("fsdp"),
        P("fsdp", None),
        P("fsdp"),
        P("fsdp", None),
        P("fsdp"),
        P("fsdp", None),
        P("fsdp"),
        P("fsdp"),
        P("fsdp"),
        P("fsdp"),
        P("fsdp"),
    )
    return jax.shard_map(body, mesh=mesh, in_specs=in_specs, out_specs=out_specs, check_vma=False)
```

profile of v0, /device:TPU:13, one launch (start us, length us, event | category | flops | bytes accessed | tf_op | source)
XLA Modules:
  0.0 4016.4 jit_solution(12273913562855665944)
XLA Ops:
  28.7 36.9 all-gather
  66.7 366.8 %all-gather.14.cloned.1.call-done = bf16[2048,6144]{1,0:T(8,128)(2,1)} async-done(((bf16[512,6144]{1,0:T(8,128)(2,1)}), bf16[2048,6144]{1,0:T(8,128)(2,1)}) %all-gather.14.cloned.1.call-update) | async-done | bytes 25165840 | tf_op jit(solution)/shard_map/all_gather | solution.py:91
  433.5 11.8 convolution_add_fusion.1
  471.4 111.5 %all-gather.20.cloned.1.call-done = bf16[2048,2048]{1,0:T(8,128)(2,1)} async-done(((bf16[512,2048]{1,0:T(8,128)(2,1)}), bf16[2048,2048]{1,0:T(8,128)(2,1)}) %all-gather.20.cloned.1.call-update) | async-done | bytes 8388624 | tf_op jit(solution)/shard_map/all_gather | solution.py:143
  595.8 25.1 all-gather.16.cloned.1.call-done
  620.9 35.9 all-gather.18.cloned.1.call-done
  656.8 34.2 while.32
  691.0 53.3 %while.33 = (s32[]{:T(128)}, f32[8,256,256]{1,2,0:T(8,128)}, bf16[8,256,1024]{2,1,0:T(8,128)(2,1)}, bf16[8,256,1024]{2,1,0:T(8,128)(2,1)}, bf16[8,256,256]{2,1,0...) while((s32[]{:T(128)}, f32[8,256,256]{1,2,0:T(8,128)}, ...), condition=%wide.region_8.9_spmd.clone.clone, body=%wide.region_6.8_spmd.clone.sunk.clone | while | flops 406126336 | bytes 10506381 | solution.py:169
  762.0 29.7 all_gather.54
  791.7 24.5 all-gather.4
  816.2 44.4 %all-gather.3 = bf16[4,1,512]{2,1,0:T(2,128)(2,1)S(1)} all-gather(bf16[1,1,512]{2,1,0:T(2,128)(2,1)S(1)} %reshape.257), channel_id=1, replica_groups=mesh['seq'=2,'ctx'=4,'fsdp'=4] {'fsdp'}, dimensions={0}, use_global_device_ids=true | all-gather | bytes 5120 | tf_op jit(solution)/shard_map/all_gather | solution.py:80
  867.6 349.4 %all-gather.22.cloned.1.call-done = bf16[2048,8192]{1,0:T(8,128)(2,1)} async-done(((bf16[512,8192]{1,0:T(8,128)(2,1)}), bf16[2048,8192]{1,0:T(8,128)(2,1)}) %all-gather.22.cloned.1.call-update) | async-done | bytes 33554448 | tf_op jit(solution)/shard_map/all_gather | solution.py:92
  1217.0 32.6 multiply_convert_fusion.1
  1249.6 16.4 convert_bitcast_fusion
  1265.9 36.8 pad_maximum_fusion.1
  1305.5 472.6 %all-gather.24.cloned.1.call-done = bf16[2048,8192]{1,0:T(8,128)(2,1)} async-done(((bf16[512,8192]{1,0:T(8,128)(2,1)}), bf16[2048,8192]{1,0:T(8,128)(2,1)}) %all-gather.24.cloned.1.call-update) | async-done | bytes 33554448 | tf_op jit(solution)/shard_map/all_gather | solution.py:144
  1778.1 33.2 convert_reduce_fusion
  1811.3 16.4 convolution_convert_fusion
  1827.7 26.2 reduce-scatter.4.cloned.1.call-done
  1857.5 15.3 convolution_convert_fusion.1
  1872.8 39.3 pad_maximum_fusion
  1912.2 17.0 fusion.104
  1929.2 14.3 fusion.95
  1953.1 586.6 %reduce-scatter.8.cloned.1.call-done = bf16[512,10240]{0,1:T(8,128)(2,1)} async-done(((bf16[2048,10240]{0,1:T(8,128)(2,1)}), bf16[512,10240]{0,1:T(8,128)(2,1)}) %reduce-scatter.8.cloned.1.call-update) | async-done | bytes 10485776 | tf_op jit(solution)/shard_map/reduce_scatter | solution.py:231
  2539.8 958.7 %reduce-scatter.6.cloned.1.call-done = bf16[512,14336]{1,0:T(8,128)(2,1)} async-done(((bf16[2048,14336]{1,0:T(8,128)(2,1)}), bf16[512,14336]{1,0:T(8,128)(2,1)}) %reduce-scatter.6.cloned.1.call-update) | async-done | bytes 14680080 | tf_op jit(solution)/shard_map/reduce_scatter | solution.py:223
  3499.2 14.2 all-gather.6
  3529.1 17.6 fusion.58
  3546.7 90.7 %all-reduce.13.cloned.1.call-done = (f32[6144]{0:T(1024)}, f32[2048]{0:T(1024)}, f32[8192]{0:T(1024)}, f32[2048]{0:T(1024)}, f32[2048]{0:T(1024)}, /*index=5*/f32[2048]{0:T(1024)}, f32[2048]{0:T(1024)}) async-done(((f32[6144]{0:T(1024)}, f32[2048]{0:T(1024)}, f32[8192]{0:T(1024)}, f32[2048]{0:T(1024)}, f32[2048]{0:T(1024)}, /*index=5*/f32[2048]{0:T(1024)}, f32[2048]{0:T(1024)}), (f32[6144]{0:T(1024)}, ...) | async-done | bytes 98320 | tf_op jit(solution)/shard_map/psum | solution.py:204
  3646.1 303.2 %all-reduce.15.cloned.1.call-done = (bf16[512,14336]{1,0:T(8,128)(2,1)}, bf16[512,10240]{0,1:T(8,128)(2,1)}) async-done(((bf16[512,14336]{1,0:T(8,128)(2,1)}, bf16[512,10240]{0,1:T(8,128)(2,1)}), (bf16[512,14336]{1,0:T(8,128)(2,1)}, bf16[512,10240]{0,1:T(8,128)(2,1)})) %all-reduce.15.cloned.1.call-update) | async-done | bytes 25165840 | tf_op jit(solution)/shard_map/psum | solution.py:240
  3958.6 11.7 slice.92
  3974.5 11.5 slice.93
  3991.4 17.4 copy.81
  (276 shorter events, 233.2 us)
Async XLA Ops:
  7.2 12.1 copy-start.27
  7.2 21.4 copy-start.28
  7.2 58.4 %copy-start.33 = (s32[1,8]{1,0:T(1,128)S(1)}, s32[1,8]{1,0:T(1,128)}, u32[]{:S(2)}) copy-start(s32[1,8]{1,0:T(1,128)} %param.20) | copy-start | bytes 100
  7.2 58.8 %copy-start = (bf16[1,256,2048]{2,1,0:T(8,128)(2,1)S(1)}, bf16[1,256,2048]{2,1,0:T(8,128)(2,1)}, u32[]{:S(2)}) copy-start(bf16[1,256,2048]{2,1,0:T(8,128)(2,1)} %param.19) | copy-start | bytes 3145732
  7.2 426.2 %all-gather.14.cloned.1.call-start = ((), (), s32[]{:S(2)}) async-start(), calls=%async_computation.3 | async-start | bytes 31457280 | tf_op jit(solution)/shard_map/all_gather | solution.py:91
  8.0 574.9 %all-gather.20.cloned.1.call-start = ((), (), s32[]{:S(2)}) async-start(), calls=%async_computation.6 | async-start | bytes 10485760 | tf_op jit(solution)/shard_map/all_gather | solution.py:143
  8.7 612.2 %all-gather.16.cloned.1.call-start = ((), (), s32[]{:S(2)}) async-start(), calls=%async_computation.4 | async-start | bytes 5242880 | tf_op jit(solution)/shard_map/all_gather | solution.py:117
  28.6 416.6 %copy-start.16 = (f32[4,1,512]{2,1,0:T(1,128)}, f32[4,1,512]{2,1,0:T(1,128)S(1)}, u32[]{:S(2)}) copy-start(f32[4,1,512]{2,1,0:T(1,128)S(1)} %convert_element_type.148) | copy-start | bytes 24580
  65.6 379.7 %copy-start.14 = (f32[4,1,512]{2,1,0:T(1,128)}, f32[4,1,512]{2,1,0:T(1,128)S(1)}, u32[]{:S(2)}) copy-start(f32[4,1,512]{2,1,0:T(1,128)S(1)} %convert_element_type.147) | copy-start | bytes 24580
  66.0 396.1 %copy-start.18 = (f32[256,64]{0,1:T(8,128)}, f32[256,64]{0,1:T(8,128)S(1)}, u32[]{:S(2)}) copy-start(f32[256,64]{0,1:T(8,128)S(1)} %get-tuple-element.372) | copy-start | bytes 196612
  66.0 396.1 %copy-start.20 = (f32[256,64]{0,1:T(8,128)}, f32[256,64]{0,1:T(8,128)S(1)}, u32[]{:S(2)}) copy-start(f32[256,64]{0,1:T(8,128)S(1)} %get-tuple-element.373) | copy-start | bytes 196612
  66.7 378.6 %copy-start.22 = (f32[256]{0:T(256)}, f32[256]{0:T(256)S(1)}, u32[]{:S(2)}) copy-start(f32[256]{0:T(256)S(1)} %fusion.65) | copy-start | bytes 3076
  465.9 190.9 %all-gather.18.cloned.1.call-start = ((), (), s32[]{:S(2)}) async-start(), calls=%async_computation.5 | async-start | bytes 5242880 | tf_op jit(solution)/shard_map/all_gather | solution.py:118
  468.8 114.1 %copy-start.3 = (bf16[1,256,2048]{2,1,0:T(8,128)(2,1)S(1)}, bf16[1,256,2048]{2,1,0:T(8,128)(2,1)}, u32[]{:S(2)}) copy-start(bf16[1,256,2048]{2,1,0:T(8,128)(2,1)} %param.33) | copy-start | bytes 3145732
  468.8 748.2 %all-gather.22.cloned.1.call-start = ((), (), s32[]{:S(2)}) async-start(), calls=%async_computation.7 | async-start | bytes 41943040 | tf_op jit(solution)/shard_map/all_gather | solution.py:92
  469.4 1308.7 %all-gather.24.cloned.1.call-start = ((), (), s32[]{:S(2)}) async-start(), calls=%async_computation.8 | async-start | bytes 41943040 | tf_op jit(solution)/shard_map/all_gather | solution.py:144
  469.9 1384.0 %reduce-scatter.4.cloned.1.call-start = ((), (), s32[]{:S(2)}) async-start(), calls=%async_computation.9 | async-start | bytes 10485760 | tf_op jit(solution)/shard_map/reduce_scatter | solution.py:177
  471.4 121.0 %copy-start.13 = (bf16[256,8,64]{0,2,1:T(8,128)(2,1)S(1)}, bf16[256,8,64]{0,2,1:T(8,128)(2,1)}, u32[]{:S(2)}) copy-start(bf16[256,8,64]{0,2,1:T(8,128)(2,1)} %get-tuple-element.367) | copy-start | bytes 786436
  761.3 30.4 copy-start.29
  761.3 54.9 %copy-start.30 = (bf16[512]{0:T(512)(128)(2,1)S(1)}, bf16[512]{0:T(512)(128)(2,1)}, u32[]{:S(2)}) copy-start(bf16[512]{0:T(512)(128)(2,1)} %param.31) | copy-start | bytes 3076
  761.3 1778.5 %reduce-scatter.8.cloned.1.call-start = ((), (), s32[]{:S(2)}) async-start(), calls=%async_computation.11 | async-start | bytes 52428800 | tf_op jit(solution)/shard_map/reduce_scatter | solution.py:231
  1302.8 2195.7 %reduce-scatter.6.cloned.1.call-start = ((), (), s32[]{:S(2)}) async-start(), calls=%async_computation.10 | async-start | bytes 73400320 | tf_op jit(solution)/shard_map/reduce_scatter | solution.py:223
  1827.7 28.2 copy-start.12
  1827.7 28.2 copy-start.21
  1827.7 28.4 copy-start.19
  1912.1 1725.2 %all-reduce.13.cloned.1.call-start = ((), (), s32[]{:S(2)}) async-start(), calls=%async_computation.12 | async-start | bytes 196608 | tf_op jit(solution)/shard_map/psum | solution.py:204
  1912.2 17.0 copy-start.2
  1929.2 14.4 copy-start.23
  1953.1 1996.3 %all-reduce.15.cloned.1.call-start = ((), (), s32[]{:S(2)}) async-start(), calls=%async_computation.13 | async-start | bytes 50331648 | tf_op jit(solution)/shard_map/psum | solution.py:240
  3498.5 14.9 copy-start.32
  3498.5 23.5 copy-start.8
  3638.1 370.7 %copy-start.24 = (f32[512]{0:T(512)}, f32[512]{0:T(512)S(1)}, u32[]{:S(2)}) copy-start(f32[512]{0:T(512)S(1)} %dynamic_slice.56) | copy-start | bytes 6148
  (13 other events, 45.4 us)
Sparse Core Ops, SparseCore 0:
  9.7 423.7 all-gather.13
  435.0 147.7 all-gather.19
  585.0 35.8 all-gather.15
  622.3 34.4 all-gather.17
  658.2 558.7 all-gather.21
  1218.4 559.5 all-gather.23
  1781.2 72.6 reduce-scatter.3
  1856.4 683.3 reduce-scatter.7
  2542.1 956.3 reduce-scatter.5
  3507.0 130.2 all-reduce.12
  3641.4 307.9 all-reduce.14
where the time goes:
time: 4030 us; the launch traced here: 4020 us
  waiting for transfers between devices  3330 us (83%)
  matrix products  271 us (7%)
  blocking collectives  178 us (4%)
  other arithmetic  114 us (3%)
  local copies, waits for them, and re-layouts  108 us (3%)
    reduce_scatter x1, waiting for transfers between devices, body(): lax.psum_scatter(jnp.concatenate([times_first(low_one, d_projected_low),...  959 us
    reduce_scatter x1, waiting for transfers between devices, body(): lax.psum_scatter(jnp.concatenate([times_first(grad_low, attended_low), ti...  587 us
    all_gather x1, waiting for transfers between devices, body(): lax.all_gather(w_down_t, 'fsdp', axis=0, tiled=True)  473 us
    all_gather x1, waiting for transfers between devices, body(): lax.all_gather(w_qkv, 'fsdp', axis=0, tiled=True)  367 us
    all_gather x1, waiting for transfers between devices, body(): lax.all_gather(w_up, 'fsdp', axis=0, tiled=True)  349 us
    psum x1, waiting for transfers between devices, body(): lax.psum(in_part.astype(jnp.bfloat16), ('seq', 'ctx')).astype(jnp.float32)  303 us
    all_gather x1, waiting for transfers between devices, body(): lax.all_gather(w_o_t, 'fsdp', axis=0, tiled=True)  111 us
    dot_general x28, matrix products, times_last(): lax.dot_general(left, right, (((1,), (1,)), ((), ())), preferred_element_...  94.6 us
  transfers between devices with their start and end apart: 11, of which 11 were waited for; matrix products, arithmetic and copies ran while one was open for 11% of the time, Pallas kernels for 0%

commit v1 on v0

v1 whole, which is shorter than its diff:
```python
import math

import jax
import jax.numpy as jnp
from jax import lax
from jax.sharding import PartitionSpec as P

HEADS = 8
HEAD = 256
ROT = 64
BLK = 128
EPS = 1e-05
PLANE = ("seq", "ctx")
LOW = jnp.bfloat16
WIDE = jnp.float32


def dot_nn(left, right):
    return lax.dot_general(left, right, (((1,), (0,)), ((), ())), preferred_element_type=WIDE)


def dot_nt(left, right):
    return lax.dot_general(left, right, (((1,), (1,)), ((), ())), preferred_element_type=WIDE)


def dot_tn(left, right):
    return lax.dot_general(left, right, (((0,), (0,)), ((), ())), preferred_element_type=WIDE)


def batch_nn(left, right):
    return lax.dot_general(left, right, (((2,), (1,)), ((0,), (0,))), preferred_element_type=WIDE)


def batch_nt(left, right):
    return lax.dot_general(left, right, (((2,), (2,)), ((0,), (0,))), preferred_element_type=WIDE)


def batch_tn(left, right):
    return lax.dot_general(left, right, (((1,), (1,)), ((0,), (0,))), preferred_element_type=WIDE)


def standardise(values):
    middle = jnp.mean(values, -1, keepdims=True)
    centred = values - middle
    spread = jnp.mean(centred * centred, -1, keepdims=True)
    scale = lax.rsqrt(spread + EPS)
    return centred * scale, scale


def angles(positions):
    freqs = 10000.0 ** (-(jnp.arange(ROT // 2, dtype=WIDE) * 2.0 / ROT))
    turned = positions.astype(WIDE)[:, None] * freqs[None, :]
    return jnp.cos(turned), jnp.sin(turned)


def turn(values, cosine, sine):
    half = ROT // 2
    one, two, rest = values[..., :half], values[..., half:ROT], values[..., ROT:]
    return jnp.concatenate([one * cosine - two * sine, two * cosine + one * sine, rest], -1)


def gelu_pair(hidden):
    bell = 0.5 * (1.0 + lax.erf(hidden * (1.0 / math.sqrt(2.0))))
    slope = bell + hidden * jnp.exp(-0.5 * hidden * hidden) * (1.0 / math.sqrt(2.0 * math.pi))
    return hidden * bell, slope


def body(tokens, block_place, w_qkv, b_qkv, w_o_t, b_o, w_up, b_up, w_down_t, b_down,
         norm1_gain, norm1_shift, norm2_gain, norm2_shift, cotangent):
    seqs, ctxs, shards = lax.axis_size("seq"), lax.axis_size("ctx"), lax.axis_size("fsdp")
    peers = seqs * ctxs
    place = lax.axis_index("seq") * ctxs + lax.axis_index("ctx")
    own, width = tokens.shape[1:]
    hidden_all = w_up.shape[1]
    length = own * ctxs
    share = max(1, peers // HEADS)
    heads = max(1, HEADS // peers)
    own_seqs = seqs // share
    group = place // share
    first_seq = (place % share) * own_seqs
    cols = heads * HEAD
    hid = hidden_all // peers

    x_own = tokens[0].astype(WIDE)
    dy_own = cotangent[0]
    both = lax.all_gather(jnp.stack([tokens[0], dy_own]), PLANE, axis=0, tiled=False)
    x_all = both[:, 0].reshape(seqs * length, width)
    dy_all = both[:, 1].reshape(seqs * length, width)
    places = lax.all_gather(block_place[0], "seq", axis=0, tiled=False)

    small = (b_qkv, b_o, b_up, b_down, norm1_gain, norm1_shift, norm2_gain, norm2_shift)
    packed = lax.all_gather(jnp.concatenate(small), "fsdp", axis=0, tiled=False)
    unpacked, start = [], 0
    for part in small:
        size = part.shape[0]
        unpacked.append(packed[:, start : start + size].reshape(-1).astype(WIDE))
        start += size
    bias_qkv, bias_o, bias_up, bias_down, gain1, shift1, gain2, shift2 = unpacked

    def head_cols(values, kinds):
        rows = values.shape[0]
        split = values.reshape(rows, kinds, HEADS * HEAD)
        return lax.dynamic_slice_in_dim(split, group * cols, cols, 2).reshape(rows, kinds * cols)

    def hid_cols(values):
        return lax.dynamic_slice_in_dim(values, place * hid, hid, 1)

    own_cols = jnp.concatenate([head_cols(w_qkv, 3), head_cols(w_o_t, 1), hid_cols(w_up), hid_cols(w_down_t)], 1)
    weights = lax.all_gather(own_cols, "fsdp", axis=0, tiled=True)
    cut = 4 * cols
    m_qkv, m_o, m_up, m_down = weights[:, : 3 * cols], weights[:, 3 * cols : cut], weights[:, cut : cut + hid], weights[:, cut + hid :]
    own_bias_qkv = head_cols(bias_qkv[None], 3)
    own_bias_up = hid_cols(bias_up[None])

    x_hat, _ = standardise(x_all.astype(WIDE))
    a1 = (x_hat * gain1 + shift1).astype(LOW)
    a2 = (x_hat * gain2 + shift2).astype(LOW)

    rows = own_seqs * length
    a1_seq = lax.dynamic_slice_in_dim(a1, first_seq * length, rows, 0)
    dy_seq = lax.dynamic_slice_in_dim(dy_all, first_seq * length, rows, 0)
    positions = (places[:, :, None] * BLK + jnp.arange(BLK, dtype=jnp.int32)).reshape(seqs, length)
    positions = lax.dynamic_slice_in_dim(positions, first_seq, own_seqs, 0)
    cosine, sine = angles(positions.reshape(-1))
    cosine, sine = cosine[:, None], sine[:, None]
    qkv = dot_nn(a1_seq, m_qkv) + own_bias_qkv

    def to_heads(values):
        return values.reshape(own_seqs, length, heads, HEAD).transpose(0, 2, 1, 3).reshape(own_seqs * heads, length, HEAD)

    def from_heads(values):
        return values.reshape(own_seqs, heads, length, HEAD).transpose(0, 2, 1, 3).reshape(rows, cols)

    def turned(values):
        return turn(values.reshape(rows, heads, HEAD), cosine, sine).reshape(rows, cols)

    def turned_back(values):
        return turn(values.reshape(rows, heads, HEAD), cosine, -sine).reshape(rows, cols)

    q = to_heads(turned(qkv[:, :cols]).astype(LOW))
    k = to_heads(turned(qkv[:, cols : 2 * cols]).astype(LOW))
    v = to_heads(qkv[:, 2 * cols :].astype(LOW))
    scaling = 1.0 / math.sqrt(HEAD)
    kept = (positions[:, :, None] >= positions[:, None, :])[:, None]
    kept = jnp.broadcast_to(kept, (own_seqs, heads, length, length)).reshape(own_seqs * heads, length, length)
    scores = jnp.where(kept, batch_nt(q, k) * scaling, -1e30)
    expo = jnp.exp(scores - jnp.max(scores, -1, keepdims=True))
    p = expo / jnp.sum(expo, -1, keepdims=True)
    p_low = p.astype(LOW)
    attn = from_heads(batch_nn(p_low, v).astype(LOW))
    d_attn = to_heads(dot_nn(dy_seq, m_o).astype(LOW))
    dp = batch_nt(d_attn, v)
    ds = jnp.where(kept, p * (dp - jnp.sum(p * dp, -1, keepdims=True)), 0.0).astype(LOW)
    dq = from_heads(batch_nn(ds, k) * scaling)
    dk = from_heads(batch_tn(ds, q) * scaling)
    dv = from_heads(batch_tn(p_low, d_attn))
    d_qkv = jnp.concatenate([turned_back(dq), turned_back(dk), dv], 1).astype(LOW)

    g, slope = gelu_pair(dot_nn(a2, m_up) + own_bias_up)
    g = g.astype(LOW)
    d_h = (dot_nn(dy_all, m_down) * slope).astype(LOW)

    def onto(values, part):
        return lax.dynamic_update_slice_in_dim(values, lax.dynamic_slice_in_dim(values, first_seq * length, rows, 0) + part, first_seq * length, 0)

    out_part = onto(dot_nt(g, m_down), dot_nt(attn, m_o))
    u_part = onto(dot_nt(d_h, m_up) * gain2, dot_nt(d_qkv, m_qkv) * gain1)
    out_sum = lax.psum_scatter(out_part.astype(LOW), PLANE, scatter_dimension=0, tiled=True).astype(WIDE)
    u_sum = lax.psum_scatter(u_part.astype(LOW), PLANE, scatter_dimension=0, tiled=True).astype(WIDE)
    output = (x_own + out_sum + bias_o + bias_down).astype(LOW)[None]
    hat_own, scale_own = standardise(x_own)
    d_x = scale_own * (u_sum - jnp.mean(u_sum, -1, keepdims=True) - hat_own * jnp.mean(u_sum * hat_own, -1, keepdims=True))
    input_grad = (dy_own.astype(WIDE) + d_x).astype(LOW)[None]

    g_qkv = dot_tn(a1_seq, d_qkv)
    g_o = dot_tn(dy_seq, attn)
    g_up = dot_tn(a2, d_h)
    g_down = dot_tn(dy_all, g)
    gb_qkv = jnp.sum(d_qkv, 0, dtype=WIDE)
    gb_up = jnp.sum(d_h, 0, dtype=WIDE)
    wide_qkv, wide_up = m_qkv.astype(WIDE), m_up.astype(WIDE)
    d_gain1 = jnp.sum(wide_qkv * (g_qkv - shift1[:, None] * gb_qkv), 1) / gain1
    d_gain2 = jnp.sum(wide_up * (g_up - shift2[:, None] * gb_up), 1) / gain2
    d_shift1 = jnp.sum(wide_qkv * gb_qkv, 1)
    d_shift2 = jnp.sum(wide_up * gb_up, 1)
    full_qkv = lax.dynamic_update_slice(jnp.zeros((3, HEADS * HEAD), WIDE), gb_qkv.reshape(3, cols), (0, group * cols)).reshape(-1)
    full_up = lax.dynamic_update_slice(jnp.zeros((hidden_all,), WIDE), gb_up, (place * hid,))
    sums = lax.psum((full_qkv, jnp.sum(dy_own, 0, dtype=WIDE), full_up, d_gain1, d_shift1, d_gain2, d_shift2), PLANE + ("fsdp",))
    mine = lax.axis_index("fsdp")

    def own_share(values):
        size = values.shape[0] // shards
        return lax.dynamic_slice_in_dim(values, mine * size, size, 0)

    sums = [own_share(s) for s in sums]
    grads = jnp.concatenate([g_qkv, g_o, g_up, g_down], 1).astype(LOW)
    reduced = lax.psum_scatter(grads, "fsdp", scatter_dimension=0, tiled=True)
    gathered = lax.all_gather(reduced, PLANE, axis=0, tiled=False)
    rows_own = reduced.shape[0]

    def spread_heads(values, kinds):
        values = values.astype(WIDE).reshape(peers // share, share, rows_own, kinds, cols).sum(1)
        return values.transpose(1, 2, 0, 3).reshape(rows_own, kinds * HEADS * HEAD)

    def spread_hid(values):
        return values.transpose(1, 0, 2).reshape(rows_own, hidden_all).astype(WIDE)

    return (
        output,
        input_grad,
        spread_heads(gathered[:, :, : 3 * cols], 3),
        sums[0],
        spread_heads(gathered[:, :, 3 * cols : cut], 1),
        sums[1],
        spread_hid(gathered[:, :, cut : cut + hid]),
        sums[2],
        spread_hid(gathered[:, :, cut + hid :]),
        sums[1],
        sums[3],
        sums[4],
        sums[5],
        sums[6],
    )


def solution(mesh):
    tok = P(("seq", "fsdp"), "ctx", None)
    mat, vec = P("fsdp", None), P("fsdp")
    params = (mat, vec, mat, vec, mat, vec, mat, vec, vec, vec, vec, vec)
    in_specs = (tok, P(("seq", "fsdp"), None)) + params + (tok,)
    return jax.shard_map(body, mesh=mesh, in_specs=in_specs, out_specs=(tok, tok) + params, check_vma=False)
```

time: 4030 us -> 1340 us (0.33)
  waiting for transfers between devices: 3330 us -> 794 us
  blocking collectives: 178 us -> 14.8 us
  local copies, waits for them, and re-layouts: 108 us -> 208 us
  matrix products: 271 us -> 206 us
    reduce_scatter x3, waiting for transfers between devices: 1570 us -> 294 us  [the longest x1 154 us: body(): reduced = lax.psum_scatter(grads, 'fsdp', scatter_dimension=0, tiled=True)]
    all_gather x6 -> x3, waiting for transfers between devices: 1360 us -> 369 us  [the longest x1 186 us: body(): weights = lax.all_gather(own_cols, 'fsdp', axis=0, tiled=True)]
    psum x2 -> x1, waiting for transfers between devices: 394 us -> 132 us  [body(): lax.psum((full_qkv, jnp.sum(dy_own, 0, dtype=WIDE), full_up, d_gain1, d_s...]
    all_gather x8 -> x2, blocking collectives: 178 us -> 14.8 us  [the longest x1 11.3 us: body(): packed = lax.all_gather(jnp.concatenate(small), 'fsdp', axis=0, tiled=False)]
    unnamed x85 -> x122, local copies, waits for them, and re-layouts: 36.3 us -> 115 us
    dot_general x54 -> x17, matrix products: 271 us -> 199 us  [the longest x4 55.1 us: dot_nt(): lax.dot_general(left, right, (((1,), (1,)), ((), ())), preferred_element_...]
    concatenate x3 -> x4, other arithmetic: 84 us -> 29.2 us  [the longest x1 27.2 us: body(): grads = jnp.concatenate([g_qkv, g_o, g_up, g_down], 1).astype(LOW)]
  transfers between devices with their start and end apart: 11 -> 7, of which waited for: 11 -> 7; matrix products, arithmetic and copies ran while one was open for 11% -> 9% of each run, Pallas kernels for 0% -> 0%
where the time goes in v1:
time: 1340 us; the launch traced here: 1330 us
  waiting for transfers between devices  794 us (59%)
  local copies, waits for them, and re-layouts  208 us (16%)
  matrix products  206 us (15%)
  other arithmetic  89.7 us (7%)
  between operations  15.1 us (1%)
  blocking collectives  14.8 us (1%)
    all_gather x1, waiting for transfers between devices, body(): weights = lax.all_gather(own_cols, 'fsdp', axis=0, tiled=True)  186 us
    reduce_scatter x1, waiting for transfers between devices, body(): reduced = lax.psum_scatter(grads, 'fsdp', scatter_dimension=0, tiled=True)  154 us
    psum x1, waiting for transfers between devices, body(): lax.psum((full_qkv, jnp.sum(dy_own, 0, dtype=WIDE), full_up, d_gain1, d_s...  132 us
    all_gather x1, waiting for transfers between devices, body(): gathered = lax.all_gather(reduced, PLANE, axis=0, tiled=False)  128 us
    unnamed x122, local copies, waits for them, and re-layouts  115 us
    reduce_scatter x1, waiting for transfers between devices, body(): lax.psum_scatter(out_part.astype(LOW), PLANE, scatter_dimension=0, tiled=...  73.1 us
    reduce_scatter x1, waiting for transfers between devices, body(): lax.psum_scatter(u_part.astype(LOW), PLANE, scatter_dimension=0, tiled=True)  66.8 us
    dot_general x4, matrix products, dot_nt(): lax.dot_general(left, right, (((1,), (1,)), ((), ())), preferred_element_...  55.1 us
  transfers between devices with their start and end apart: 7, of which 7 were waited for; matrix products, arithmetic and copies ran while one was open for 9% of the time, Pallas kernels for 0%

profile of v1, /device:TPU:13, one launch (start us, length us, event | category | flops | bytes accessed | tf_op | source)
XLA Modules:
  0.0 1328.1 jit_solution(13922121956261513399)
XLA Ops:
  17.0 9.0 copy.70
  34.1 11.3 all-gather.3
  46.3 54.9 %all-gather.11.cloned.1.call-done = bf16[16,256,2048]{2,1,0:T(8,128)(2,1)} async-done(((bf16[2,256,2048]{2,1,0:T(8,128)(2,1)}), bf16[16,256,2048]{2,1,0:T(8,128)(2,1)}) %all-gather.11.cloned.1.call-update) | async-done | bytes 16777232 | tf_op jit(solution)/shard_map/all_gather | solution.py:86
  101.3 8.4 slice.159
  121.5 11.6 add_convert_fusion.2
  133.1 186.1 %all-gather.9.cloned.1.call-done = bf16[2048,3072]{0,1:T(8,128)(2,1)} async-done(((bf16[512,3072]{0,1:T(8,128)(2,1)}), bf16[2048,3072]{0,1:T(8,128)(2,1)}) %all-gather.9.cloned.1.call-update) | async-done | bytes 12582928 | tf_op jit(solution)/shard_map/all_gather | solution.py:109
  319.2 10.1 broadcast_add_fusion
  359.3 15.0 %fusion.58 = f32[2,1024,256]{2,1,0:T(8,128)} fusion(bf16[2,1024,256]{2,1,0:T(8,128)(2,1)S(1)} %bitcast.212, f32[2,1024,1024]{1,2,0:T(8,128)} %fusion.115, s32[2,1024]{1,0:T(2,128)S(1)} %bitcast_add_fusion, f32[2,1024,1024]{1,2,0:T(8,128)} %get-tuple-element.64, f32[2,1024]{1,0:T(2,128)S(1)} %get-tuple-element.63), kind=kOutput, calls=%fused_computation.96 | convolution fusion | flops 1091046400 | bytes 19939328 | tf_op jit(solution)/shard_map/dot_general | solution.py:39
  374.3 15.1 %fusion.55 = f32[2,1024,256]{2,1,0:T(8,128)S(1)} fusion(bf16[2,1024,256]{2,1,0:T(8,128)(2,1)} %bitcast.214, f32[2,1024,1024]{1,2,0:T(8,128)} %fusion.115, s32[2,1024]{1,0:T(2,128)S(1)} %bitcast_add_fusion, f32[2,1024,1024]{1,2,0:T(8,128)} %get-tuple-element.64, f32[2,1024]{1,0:T(2,128)S(1)} %get-tuple-element.63), kind=kOutput, calls=%fused_computation.95 | convolution fusion | flops 1091046400 | bytes 19939328 | tf_op jit(solution)/shard_map/dot_general | solution.py:31
  416.4 15.2 %multiply_convert_fusion = (bf16[2048,1024]{1,0:T(8,128)(2,1)S(1)}, f32[2048,1024]{1,0:T(8,128)}) fusion(f32[1024]{0:T(1024)S(1)} %dynamic-slice.4, bf16[2048,2048]{1,0:T(8,128)(2,1)} %get-tuple-element.30, bf16[2048,3072]{0,1:T(8,128)(2,1)} %all-gather.9.cloned.1.call-done), kind=kOutput, calls=%fused_computation.32 | convolution fusion | flops 8602517504 | bytes 25169920 | tf_op jit(solution)/shard_map/dot_general | solution.py:19
  431.6 13.3 %convolution_convert_fusion = bf16[2048,1024]{0,1:T(8,128)(2,1)S(1)} fusion(bf16[2048,2048]{1,0:T(8,128)(2,1)} %bitcast.194, bf16[2048,1024]{1,0:T(8,128)(2,1)S(1)} %get-tuple-element.65), kind=kOutput, calls=%fused_computation.46 | convolution fusion | flops 8592031744 | bytes 16777216 | tf_op jit(solution)/shard_map/dot_general | solution.py:27
  453.9 17.2 %convert_reduce_fusion.1 = (f32[1024]{0:T(1024)S(1)}, bf16[2048,1024]{1,0:T(8,128)(2,1)}) fusion(f32[2048,1024]{1,0:T(8,128)} %get-tuple-element.66, f32[1024]{0:T(1024)S(1)} %dynamic-slice.4, bf16[2048,2048]{1,0:T(8,128)(2,1)S(1)} %bitcast.198, bf16[2048,3072]{0,1:T(8,128)(2,1)} %all-gather.9.cloned.1.call-done), kind=kOutput, calls=%fused_computation.28 | convolution fusion | flops 8617196544 | bytes 25174016 | tf_op jit(solution)/shard_map/dot_general | solution.py:19
  471.1 14.1 %fusion.14 = (f32[2048]{0:T(1024)}, f32[2048]{0:T(1024)S(1)}, bf16[2048,768]{0,1:T(8,128)(2,1)S(1)}) fusion(f32[768]{0:T(1024)S(1)} %convert_reduce_fusion.2, bf16[2048,3072]{0,1:T(8,128)(2,1)} %all-gather.9.cloned.1.call-done, f32[2048]{0:T(1024)S(1)} %bitcast.230, bf16[2048,2048]{1,0:T(8,128)(2,1)} %get-tuple-element.29, bf16[2048,256]{0,1:T(8,128)(2,1)S(1)} %copy.93, ...), kind=kOutput, calls=%fused_computation.37 | convolution fusion | flops 6464466944 | bytes 17853440 | tf_op jit(solution)/shard_map/dot_general | solution.py:27
  485.2 14.7 %fusion.4 = (f32[2048]{0:T(1024)}, f32[2048]{0:T(1024)S(1)}, bf16[2048,1024]{0,1:T(8,128)(2,1)S(1)}) fusion(f32[1024]{0:T(1024)S(1)} %get-tuple-element.67, bf16[2048,3072]{0,1:T(8,128)(2,1)} %all-gather.9.cloned.1.call-done, f32[2048]{0:T(1024)S(1)} %bitcast.228, bf16[2048,2048]{1,0:T(8,128)(2,1)} %get-tuple-element.30, bf16[2048,1024]{1,0:T(8,128)(2,1)S(1)} %copy-done.39), kind=kOutput, calls=%fused_computation.19 | convolution fusion | flops 8606707712 | bytes 21000192 | tf_op jit(solution)/shard_map/dot_general | solution.py:27
  500.0 27.2 %pad_maximum_fusion = bf16[2048,3072]{0,1:T(8,128)(2,1)} fusion(bf16[2048,1024]{0,1:T(8,128)(2,1)S(1)} %convolution_convert_fusion, bf16[2048,1024]{0,1:T(8,128)(2,1)S(1)} %get-tuple-element.31, bf16[2048,256]{0,1:T(8,128)(2,1)S(1)} %copy-done.12, bf16[2048,768]{0,1:T(8,128)(2,1)S(1)} %get-tuple-element.32), kind=kLoop, calls=%fused_computation.12 | loop fusion | flops 50331648 | bytes 25165824 | tf_op jit(solution)/shard_map/concatenate | solution.py:196
  531.3 12.3 fusion.52
  543.6 15.4 %add_convert_fusion = bf16[2048,2048]{1,0:T(8,128)(2,1)} fusion(f32[2048,2048]{1,0:T(8,128)} %fusion.52, bf16[2048,1024]{1,0:T(8,128)(2,1)S(1)} %copy-done.40, f32[2048]{0:T(1024)S(1)} %bitcast.222, f32[2048]{0:T(1024)S(1)} %bitcast.225, bf16[2048,3072]{0,1:T(8,128)(2,1)} %all-gather.9.cloned.1.call-done), kind=kOutput, calls=%fused_computation.6 | convolution fusion | flops 8606711808 | bytes 33570816 | tf_op jit(solution)/shard_map/dot_general | solution.py:23
  559.0 15.6 %fusion.23 = f32[2048,2048]{1,0:T(8,128)} fusion(bf16[2048,1024]{1,0:T(8,128)(2,1)} %copy-done.41, bf16[2048,3072]{0,1:T(8,128)(2,1)} %all-gather.9.cloned.1.call-done), kind=kOutput, calls=%fused_computation.48 | convolution fusion | flops 8589934592 | bytes 25165824 | tf_op jit(solution)/shard_map/dot_general | solution.py:23
  574.6 11.9 add_convert_fusion.1
  586.6 153.6 %reduce-scatter.8.cloned.1.call-done = bf16[512,3072]{0,1:T(8,128)(2,1)} async-done(((bf16[2048,3072]{0,1:T(8,128)(2,1)}), bf16[512,3072]{0,1:T(8,128)(2,1)}) %reduce-scatter.8.cloned.1.call-update) | async-done | bytes 3145744 | tf_op jit(solution)/shard_map/reduce_scatter | solution.py:197
  740.9 131.6 %all-reduce.3.cloned.1.call-done = (f32[6144]{0:T(1024)}, f32[2048]{0:T(1024)}, f32[8192]{0:T(1024)}, f32[2048]{0:T(1024)}, f32[2048]{0:T(1024)}, /*index=5*/f32[2048]{0:T(1024)}, f32[2048]{0:T(1024)}) async-done(((f32[6144]{0:T(1024)}, f32[2048]{0:T(1024)}, f32[8192]{0:T(1024)}, f32[2048]{0:T(1024)}, f32[2048]{0:T(1024)}, /*index=5*/f32[2048]{0:T(1024)}, f32[2048]{0:T(1024)}), (f32[6144]{0:T(1024)}, ...) | async-done | bytes 98320 | tf_op jit(solution)/shard_map/psum | solution.py:188
  881.3 66.8 %reduce-scatter.6.cloned.1.call-done = bf16[256,2048]{1,0:T(8,128)(2,1)} async-done(((bf16[2048,2048]{1,0:T(8,128)(2,1)}), bf16[256,2048]{1,0:T(8,128)(2,1)}) %reduce-scatter.6.cloned.1.call-update) | async-done | bytes 1048592 | tf_op jit(solution)/shard_map/reduce_scatter | solution.py:169
  950.0 73.1 %reduce-scatter.4.cloned.1.call-done = bf16[256,2048]{1,0:T(8,128)(2,1)} async-done(((bf16[2048,2048]{1,0:T(8,128)(2,1)}), bf16[256,2048]{1,0:T(8,128)(2,1)}) %reduce-scatter.4.cloned.1.call-update) | async-done | bytes 1048592 | tf_op jit(solution)/shard_map/reduce_scatter | solution.py:168
  1027.2 127.6 %all-gather.13.cloned.1.call-done = bf16[4096,3072]{0,1:T(8,128)(2,1)} async-done(((bf16[512,3072]{0,1:T(8,128)(2,1)}), bf16[4096,3072]{0,1:T(8,128)(2,1)}) %all-gather.13.cloned.1.call-update) | async-done | bytes 25165840 | tf_op jit(solution)/shard_map/all_gather | solution.py:198
  1154.9 24.4 %copy.118 = bf16[384,8,8,512]{3,2,1,0:T(8,128)(2,1)} copy(bf16[384,8,8,512]{3,1,2,0:T(8,128)(2,1)} %bitcast.187) | data formatting | bytes 50331648
  1189.4 17.3 %convert_bitcast_fusion = (f32[512,8,1024]{0,1,2:T(8,128)}, f32[512,8,1024]{0,1,2:T(8,128)}) fusion(bf16[8,512,3072]{1,0,2:T(8,128)(2,1)} %bitcast.179), kind=kLoop, calls=%fused_computation.4 | loop fusion | flops 8388608 | bytes 50331648 | tf_op jit(solution)/shard_map/convert_element_type | solution.py:206
  1206.7 10.6 copy.85
  1217.4 15.2 %copy.119 = f32[64,8,24,256]{3,1,2,0:T(8,128)} copy(f32[64,8,24,256]{3,2,1,0:T(8,128)} %bitcast.186) | data formatting | bytes 25165824
  1244.2 16.9 %copy.87 = f32[512,8,1024]{2,1,0:T(8,128)} copy(f32[512,8,1024]{0,1,2:T(8,128)} %get-tuple-element.28) | data formatting | bytes 33554432 | tf_op jit(solution)/shard_map/convert_element_type | solution.py:206
  1261.1 21.2 %copy.121 = f32[64,8,8,1024]{3,1,2,0:T(8,128)} copy(f32[64,8,8,1024]{3,2,1,0:T(8,128)} %bitcast.184) | data formatting | bytes 33554432
  1282.3 16.6 %copy.88 = f32[512,8,1024]{2,1,0:T(8,128)} copy(f32[512,8,1024]{0,1,2:T(8,128)} %get-tuple-element.27) | data formatting | bytes 33554432 | tf_op jit(solution)/shard_map/convert_element_type | solution.py:206
  1299.0 21.4 %copy.122 = f32[64,8,8,1024]{3,1,2,0:T(8,128)} copy(f32[64,8,8,1024]{3,2,1,0:T(8,128)} %bitcast.185) | data formatting | bytes 33554432
  (208 shorter events, 138.0 us)
Async XLA Ops:
  7.2 9.6 copy-start
  7.2 94.1 %all-gather.11.cloned.1.call-start = ((), (), s32[]{:S(2)}) async-start(), calls=%async_computation.7 | async-start | bytes 18874368 | tf_op jit(solution)/shard_map/all_gather | solution.py:86
  10.5 308.8 %all-gather.9.cloned.1.call-start = ((), (), s32[]{:S(2)}) async-start(), calls=%async_computation.3 | async-start | bytes 15728640 | tf_op jit(solution)/shard_map/all_gather | solution.py:109
  16.8 10.6 copy-start.8
  16.8 10.5 copy-start.9
  29.2 711.0 %reduce-scatter.8.cloned.1.call-start = ((), (), s32[]{:S(2)}) async-start(), calls=%async_computation.6 | async-start | bytes 15728640 | tf_op jit(solution)/shard_map/reduce_scatter | solution.py:197
  46.1 75.3 %copy-start.25 = (f32[1,4,4,128]{3,1,2,0:T(4,128)}, f32[1,4,4,128]{3,1,2,0:T(4,128)S(1)}, u32[]{:S(2)}) copy-start(f32[1,4,4,128]{3,1,2,0:T(4,128)S(1)} %copy.115) | copy-start | bytes 24580
  46.1 75.3 %copy-start.19 = (f32[1,4,4,128]{3,1,2,0:T(4,128)}, f32[1,4,4,128]{3,1,2,0:T(4,128)S(1)}, u32[]{:S(2)}) copy-start(f32[1,4,4,128]{3,1,2,0:T(4,128)S(1)} %copy.114) | copy-start | bytes 24580
  46.1 75.3 %copy-start.23 = (f32[1,4,4,128]{3,1,2,0:T(4,128)}, f32[1,4,4,128]{3,1,2,0:T(4,128)S(1)}, u32[]{:S(2)}) copy-start(f32[1,4,4,128]{3,1,2,0:T(4,128)S(1)} %copy.111) | copy-start | bytes 24580
  46.2 75.3 %copy-start.21 = (f32[1,4,4,128]{3,1,2,0:T(4,128)}, f32[1,4,4,128]{3,1,2,0:T(4,128)S(1)}, u32[]{:S(2)}) copy-start(f32[1,4,4,128]{3,1,2,0:T(4,128)S(1)} %copy.110) | copy-start | bytes 24580
  404.8 10.4 copy-start.4
  416.4 37.5 %slice-start = ((s8[8388608]{0:T(1024)(128)(4,1)}), s8[4194304]{0:T(1024)(128)(4,1)S(1)}, s32[]{:S(2)}) async-start(s8[8388608]{0:T(1024)(128)(4,1)} %bitcast.196), calls=%async_computation.10 | async-start | bytes 8388608
  431.6 13.3 %copy-start.41 = (bf16[2048,1024]{1,0:T(8,128)(2,1)}, bf16[2048,1024]{1,0:T(8,128)(2,1)S(1)}, u32[]{:S(2)}) copy-start(bf16[2048,1024]{1,0:T(8,128)(2,1)S(1)} %get-tuple-element.65) | copy-start | bytes 12582916
  431.6 13.3 %copy-start.16 = (bf16[2,1024,256]{2,1,0:T(8,128)(2,1)S(1)}, bf16[2,1024,256]{2,1,0:T(8,128)(2,1)}, u32[]{:S(2)}) copy-start(bf16[2,1024,256]{2,1,0:T(8,128)(2,1)} %fusion.61) | copy-start | bytes 3145732
  431.6 22.3 %slice-start.1 = ((s8[8388608]{0:T(1024)(128)(4,1)}), s8[4194304]{0:T(1024)(128)(4,1)S(1)}, s32[]{:S(2)}) async-start(s8[8388608]{0:T(1024)(128)(4,1)} %bitcast.196), calls=%async_computation.11 | async-start | bytes 8388608
  444.9 8.2 copy-start.11
  453.3 17.8 %copy-start.6 = (bf16[2048,256]{0,1:T(8,128)(2,1)}, bf16[2048,256]{0,1:T(8,128)(2,1)S(1)}, u32[]{:S(2)}) copy-start(bf16[2048,256]{0,1:T(8,128)(2,1)S(1)} %maximum_bitcast_fusion) | copy-start | bytes 3145732
  453.9 17.2 %copy-start.26 = (f32[1,4,4,128]{3,1,2,0:T(4,128)S(1)}, f32[1,4,4,128]{3,1,2,0:T(4,128)}, u32[]{:S(2)}) copy-start(f32[1,4,4,128]{3,1,2,0:T(4,128)} %copy-done.25) | copy-start | bytes 24580
  471.1 14.1 %copy-start.24 = (f32[1,4,4,128]{3,1,2,0:T(4,128)S(1)}, f32[1,4,4,128]{3,1,2,0:T(4,128)}, u32[]{:S(2)}) copy-start(f32[1,4,4,128]{3,1,2,0:T(4,128)} %copy-done.23) | copy-start | bytes 24580
  471.1 14.1 %copy-start.39 = (bf16[2048,1024]{1,0:T(8,128)(2,1)S(1)}, bf16[2048,1024]{1,0:T(8,128)(2,1)}, u32[]{:S(2)}) copy-start(bf16[2048,1024]{1,0:T(8,128)(2,1)} %get-tuple-element.68) | copy-start | bytes 12582916
  485.2 14.7 %copy-start.12 = (bf16[2048,256]{0,1:T(8,128)(2,1)S(1)}, bf16[2048,256]{0,1:T(8,128)(2,1)}, u32[]{:S(2)}) copy-start(bf16[2048,256]{0,1:T(8,128)(2,1)} %convolution_convert_fusion.1) | copy-start | bytes 3145732
  527.2 345.3 %all-reduce.3.cloned.1.call-start = ((), (), s32[]{:S(2)}) async-start(), calls=%async_computation.9 | async-start | bytes 196608 | tf_op jit(solution)/shard_map/psum | solution.py:188
  531.2 416.8 %reduce-scatter.6.cloned.1.call-start = ((), (), s32[]{:S(2)}) async-start(), calls=%async_computation.5 | async-start | bytes 9437184 | tf_op jit(solution)/shard_map/reduce_scatter | solution.py:169
  531.3 12.3 copy-start.40
  558.9 15.6 %copy-start.17 = (bf16[2,1024,256]{2,1,0:T(8,128)(2,1)S(1)}, bf16[2,1024,256]{2,1,0:T(8,128)(2,1)}, u32[]{:S(2)}) copy-start(bf16[2,1024,256]{2,1,0:T(8,128)(2,1)} %fusion.61) | copy-start | bytes 3145732
  559.0 464.2 %reduce-scatter.4.cloned.1.call-start = ((), (), s32[]{:S(2)}) async-start(), calls=%async_computation.4 | async-start | bytes 9437184 | tf_op jit(solution)/shard_map/reduce_scatter | solution.py:168
  586.5 153.7 %copy-start.28 = (f32[1,4,4,128]{3,2,1,0:T(4,128)S(1)}, f32[1,4,4,128]{3,2,1,0:T(4,128)}, u32[]{:S(2)}) copy-start(f32[1,4,4,128]{3,2,1,0:T(4,128)} %get-tuple-element.50) | copy-start | bytes 24580
  586.5 153.8 %copy-start.27 = (f32[1,4,4,128]{3,2,1,0:T(4,128)S(1)}, f32[1,4,4,128]{3,2,1,0:T(4,128)}, u32[]{:S(2)}) copy-start(f32[1,4,4,128]{3,2,1,0:T(4,128)} %get-tuple-element.49) | copy-start | bytes 24580
  586.5 153.8 %copy-start.2 = (bf16[1,256,2048]{2,1,0:T(8,128)(2,1)S(1)}, bf16[1,256,2048]{2,1,0:T(8,128)(2,1)}, u32[]{:S(2)}) copy-start(bf16[1,256,2048]{2,1,0:T(8,128)(2,1)} %param.15) | copy-start | bytes 3145732
  586.5 568.4 %all-gather.13.cloned.1.call-start = ((), (), s32[]{:S(2)}) async-start(), calls=%async_computation.8 | async-start | bytes 28311552 | tf_op jit(solution)/shard_map/all_gather | solution.py:198
  873.3 447.1 %copy-start.29 = (f32[512]{0:T(512)}, f32[512]{0:T(512)S(1)}, u32[]{:S(2)}) copy-start(f32[512]{0:T(512)S(1)} %dynamic_slice.45) | copy-start | bytes 6148
  1299.0 22.0 %copy-start.1 = (bf16[512,2048]{1,0:T(8,128)(2,1)S(1)}, bf16[512,2048]{1,0:T(8,128)(2,1)}, u32[]{:S(2)}) copy-start(bf16[512,2048]{1,0:T(8,128)(2,1)} %param.19) | copy-start | bytes 6291460
  (19 other events, 107.4 us)
Sparse Core Ops, SparseCore 0:
  10.6 90.6 all-gather.10
  103.4 215.7 all-gather.8
  527.3 212.8 reduce-scatter.7
  747.0 125.4 all-reduce.2
  876.4 71.6 reduce-scatter.5
  951.8 71.2 reduce-scatter.3
  1025.0 129.8 all-gather.12

commit v2 on v1

--- a/solution.py
+++ b/solution.py
@@ -3,6 +3,8 @@
 import jax
 import jax.numpy as jnp
 from jax import lax
+from jax.experimental import pallas as pl
+from jax.experimental.pallas import tpu as pltpu
 from jax.sharding import PartitionSpec as P
 
 HEADS = 8
@@ -223,9 +225,462 @@
     )
 
 
+MESH = pl.DeviceIdType.MESH
+PIECES = 12
+ROWS = 512
+COLS = 256
+WIDTH = 2048
+TOK = 2048
+LENGTH = 1024
+HOPS = 3
+AG_SLOTS = 36
+RS_START = 20
+RING = 6
+SCALING = 1.0 / math.sqrt(HEAD)
+
+
+def fits(mesh):
+    return dict(mesh.shape) == {"seq": 2, "ctx": 4, "fsdp": 4}
+
+
+def at(index, size):
+    return pl.ds(pl.multiple_of(index * size, size), size)
+
+
+def layer_kernel(x_hbm, dy_hbm, w_qkv, w_o, w_up, w_down, table, pos_row, rows_in, bias_in, cols_in,
+                 red_out, out_out, u_out, small_out, gb_out,
+                 w_all, act, x_buf, dy_buf, g_ring, landing, red_buf, small, gb, dk_acc, dv_acc, tab, pos, rows, bias,
+                 load_sem, own_sem, ag_send, ag_recv, rs_send, rs_recv, red_sem):
+    y, c, z = lax.axis_index("seq"), lax.axis_index("ctx"), lax.axis_index("fsdp")
+    place = y * 4 + c
+    right, left = (y, c, jnp.minimum(z + 1, 3)), (y, c, jnp.maximum(z - 1, 0))
+
+    barrier = pltpu.get_barrier_semaphore()
+
+    @pl.when(z < 3)
+    def _():
+        pl.semaphore_signal(barrier, inc=1, device_id=right, device_id_type=MESH)
+
+    @pl.when(z > 0)
+    def _():
+        pl.semaphore_signal(barrier, inc=1, device_id=left, device_id_type=MESH)
+
+    def own_piece(i):
+        if i < 3:
+            source = w_qkv.at[:, at(i * 8 + place, COLS)]
+        elif i == 3:
+            source = w_o.at[:, at(place, COLS)]
+        else:
+            source = (w_up if i % 2 == 0 else w_down).at[:, at(place * 4 + (i - 4) // 2, COLS)]
+        return pltpu.make_async_copy(source, w_all.at[i, at(z, ROWS)], own_sem.at[i])
+
+    for i in range(PIECES):
+        own_piece(i).start()
+    loads = [
+        pltpu.make_async_copy(x_hbm, x_buf, load_sem.at[0]),
+        pltpu.make_async_copy(dy_hbm, dy_buf, load_sem.at[1]),
+        pltpu.make_async_copy(table, tab, load_sem.at[2]),
+        pltpu.make_async_copy(pos_row, pos, load_sem.at[3]),
+        pltpu.make_async_copy(rows_in, rows, load_sem.at[4]),
+        pltpu.make_async_copy(bias_in, bias, load_sem.at[5]),
+        pltpu.make_async_copy(cols_in, small, load_sem.at[6]),
+    ]
+    for load in loads:
+        load.start()
+    for i in range(PIECES):
+        own_piece(i).wait()
+    pl.semaphore_wait(barrier, jnp.where((z > 0) & (z < 3), 2, 1))
+
+    def ag_copy(way, piece, hop, shard):
+        block = w_all.at[piece, at(shard, ROWS)]
+        return pltpu.make_async_remote_copy(
+            src_ref=block, dst_ref=block, send_sem=ag_send.at[way, piece, hop], recv_sem=ag_recv.at[way, piece, hop],
+            device_id=right if way == 0 else left, device_id_type=MESH)
+
+    def ag_service(slot):
+        before = slot - 2
+
+        def parts(s):
+            return (s // 6) * 2 + s % 2, (s // 2) % 3
+
+        old, old_hop = parts(jnp.maximum(before, 0))
+        live = (before >= 0) & (before < AG_SLOTS)
+
+        @pl.when(live & (z >= 1) & (z - 1 - old_hop >= 0))
+        def _():
+            ag_copy(0, old, old_hop, z - 1 - old_hop).wait_recv()
+
+        @pl.when(live & (z <= 2) & (z + 1 + old_hop <= 3))
+        def _():
+            ag_copy(1, old, old_hop, z + 1 + old_hop).wait_recv()
+
+        piece, hop = parts(jnp.minimum(slot, AG_SLOTS - 1))
+
+        @pl.when((slot < AG_SLOTS) & (z <= 2) & (z - hop >= 0))
+        def _():
+            ag_copy(0, piece, hop, z - hop).start()
+
+        @pl.when((slot < AG_SLOTS) & (z >= 1) & (z + hop <= 3))
+        def _():
+            ag_copy(1, piece, hop, z + hop).start()
+
+        @pl.when(live & (z <= 2) & (z - old_hop >= 0))
+        def _():
+            ag_copy(0, old, old_hop, z - old_hop).wait_send()
+
+        @pl.when(live & (z >= 1) & (z + old_hop <= 3))
+        def _():
+            ag_copy(1, old, old_hop, z + old_hop).wait_send()
+
+    def rs_piece(n):
+        return jnp.where(n < 4, 3 - n, n)
+
+    def rs_copy(way, n, hop, shard):
+        return pltpu.make_async_remote_copy(
+            src_ref=g_ring.at[n % RING, at(shard, ROWS)], dst_ref=landing.at[way, n % 4, hop],
+            send_sem=rs_send.at[way, n, hop], recv_sem=rs_recv.at[way, n, hop],
+            device_id=right if way == 0 else left, device_id_type=MESH)
+
+    def rs_add(way, n, hop, shard):
+        rs_copy(way, n, hop, shard).wait_recv()
+        block = g_ring.at[n % RING, at(shard, ROWS)]
+        block[...] = (block[...].astype(WIDE) + landing[way, n % 4, hop].astype(WIDE)).astype(LOW)
+
+    def red_copy(n):
+        return pltpu.make_async_copy(red_buf.at[n % 4], red_out.at[rs_piece(n)], red_sem.at[n])
+
+    def rs_service(slot):
+        before = slot - 2
+
+        def parts(s):
+            return (s // 6) * 2 + s % 2, (s // 2) % 3
+
+        old, old_hop = parts(jnp.clip(before, 0, AG_SLOTS - 1))
+        live = (before >= 0) & (before < AG_SLOTS)
+
+        @pl.when(live & (z >= 1) & (z - 1 <= old_hop))
+        def _():
+            rs_add(0, old, old_hop, z + 2 - old_hop)
+
+        @pl.when(live & (z <= 2) & (2 - z <= old_hop))
+        def _():
+            rs_add(1, old, old_hop, z - 2 + old_hop)
+
+        @pl.when(live & (z <= 2) & (z <= old_hop))
+        def _():
+            rs_copy(0, old, old_hop, z + 3 - old_hop).wait_send()
+
+        @pl.when(live & (z >= 1) & (3 - z <= old_hop))
+        def _():
+            rs_copy(1, old, old_hop, z - 3 + old_hop).wait_send()
+
+        piece, hop = parts(jnp.clip(slot, 0, AG_SLOTS - 1))
+        sending = (slot >= 0) & (slot < AG_SLOTS)
+
+        @pl.when(sending & (z <= 2) & (z <= hop))
+        def _():
+            rs_copy(0, piece, hop, z + 3 - hop).start()
+
+        @pl.when(sending & (z >= 1) & (3 - z <= hop))
+        def _():
+            rs_copy(1, piece, hop, z - 3 + hop).start()
+
+        @pl.when(live & (old_hop == 2))
+        def _():
+            @pl.when(old >= 4)
+            def _():
+                red_copy(old - 4).wait()
+
+            red_buf[old % 4] = g_ring[old % RING, at(z, ROWS)]
+            red_copy(old).start()
+
+    def service(slot):
+        if isinstance(slot, int):
+            if slot < AG_SLOTS + 2:
+                ag_service(jnp.int32(slot))
+            if slot >= RS_START:
+                rs_service(jnp.int32(slot - RS_START))
+        else:
+            ag_service(slot)
+            rs_service(slot - RS_START)
+
+    def loop(count, body, first=None):
+        def step(i, carry):
+            if first is not None:
+                service(first + i)
+            body(i)
+            return carry
+
+        lax.fori_loop(0, count, step, 0)
+
+    def norm_tile(which):
+        def run(i):
+            def part(n, carry):
+                block = at(i * 4 + n, 64)
+                centred, scale = standardise_rows(x_buf[block, :].astype(WIDE))
+                x_buf[block, :] = (centred * scale * rows[2 * which : 2 * which + 1, :] + rows[2 * which + 1 : 2 * which + 2, :]).astype(LOW)
+                return carry
+
+            lax.fori_loop(0, 4, part, 0)
+        return run
+
+    loads[0].wait()
+    for load in loads[2:]:
+        load.wait()
+    loop(8, norm_tile(0), 0)
+
+    lane = lax.broadcasted_iota(jnp.int32, (1, 128), 1)
+
+    def turned(values, block, sign):
+        entry = tab[block, :]
+        cosine = jnp.where(lane < 32, entry, jnp.where(lane < 64, pltpu.roll(entry, 32, 1), 1.0))
+        sine = jnp.where(lane < 32, -pltpu.roll(entry, 96, 1), jnp.where(lane < 64, entry, 0.0))
+        low = values[:, :128]
+        partner = jnp.where(lane < 32, pltpu.roll(low, 96, 1), pltpu.roll(low, 32, 1))
+        return jnp.concatenate([low * cosine + partner * (sine * sign), values[:, 128:]], 1)
+
+    def project(kind):
+        def run(i):
+            block = at(i, 512)
+            made = dot_nn(x_buf[block, :], w_all[kind]) + bias[kind : kind + 1, :]
+            if kind < 2:
+                made = turned(made, block, 1.0)
+            act[9 + kind, block, :] = made.astype(LOW)
+        return run
+
+    loop(4, project(0), 8)
+    loop(4, project(1))
+    loop(4, project(2), 12)
+    loads[1].wait()
+
+    def attend(i):
+        seq = i // 4
+        block, keys = at(i, 256), at(seq, LENGTH)
+
+        @pl.when(i % 4 == 0)
+        def _():
+            dk_acc[...] = jnp.zeros_like(dk_acc)
+            dv_acc[...] = jnp.zeros_like(dv_acc)
+
+        q, k, v = act[9, block, :], act[10, keys, :], act[11, keys, :]
+        kept = tab[block, 64:65] >= pos[pl.ds(seq, 1), :]
+        scores = jnp.where(kept, dot_nt(q, k) * SCALING, -1e30)
+        expo = jnp.exp(scores - jnp.max(scores, -1, keepdims=True))
+        p = expo * (1.0 / jnp.sum(expo, -1, keepdims=True))
+        p_low = p.astype(LOW)
+        act[3, block, :] = dot_nn(p_low, v).astype(LOW)
+        d_attn = dot_nn(dy_buf[block, :], w_all[3]).astype(LOW)
+        dp = dot_nt(d_attn, v)
+        ds = jnp.where(kept, p * (dp - jnp.sum(p * dp, -1, keepdims=True)), 0.0).astype(LOW)
+        act[0, block, :] = turned(dot_nn(ds, k) * SCALING, block, -1.0).astype(LOW)
+        dk_acc[...] += dot_tn(ds, q)
+        dv_acc[...] += dot_tn(p_low, d_attn)
+
+        @pl.when(i % 4 == 3)
+        def _():
+            act[1, keys, :] = turned(dk_acc[...] * SCALING, keys, -1.0).astype(LOW)
+            act[2, keys, :] = dv_acc[...].astype(LOW)
+
+    def attend_two(i):
+        attend(2 * i)
+        attend(2 * i + 1)
+
+    loop(4, attend_two, 16)
+
+    def gradient(piece, n, source):
+        def run():
+            if piece != 3 and (piece < 3 or piece % 2 == 0):
+                gb[piece : piece + 1, :] = jnp.sum(act[piece].astype(WIDE), 0, keepdims=True)
+
+            def part(s, carry):
+                block = at(s, ROWS)
+                made = dot_tn(source[:, block], act[piece])
+                g_ring[n % RING, block, :] = made.astype(LOW)
+                if piece < 3 or (piece != 3 and piece % 2 == 0):
+                    mine = 0 if piece < 3 else 1
+                    weight = w_all[piece, block, :].astype(WIDE)
+                    sums = gb[piece : piece + 1, :]
+                    gain = jnp.sum(weight * (made - small[block, mine : mine + 1] * sums), 1, keepdims=True)
+                    shift = jnp.sum(weight * sums, 1, keepdims=True)
+                    here = 8 + 2 * mine
+                    old = small[block, :]
+                    small[block, :] = old + jnp.where(lane == here, gain, 0.0) + jnp.where(lane == here + 1, shift, 0.0)
+                return carry
+
+            lax.fori_loop(0, 4, part, 0)
+        return run
+
+    gradient(3, 0, dy_buf)()
+    gradient(2, 1, x_buf)()
+    service(20)
+    gradient(1, 2, x_buf)()
+    service(21)
+    gradient(0, 3, x_buf)()
+    service(22)
+    again = pltpu.make_async_copy(x_hbm, x_buf, load_sem.at[0])
+    again.start()
+    again.wait()
+    service(23)
+    loop(4, norm_tile(1), 24)
+    loop(4, lambda i: norm_tile(1)(i + 4))
+
+    def feed(part):
+        up, down = 4 + 2 * part, 5 + 2 * part
+
+        def run(i):
+            block = at(i, 512)
+            hidden = dot_nn(x_buf[block, :], w_all[up]) + bias[3 + part : 4 + part, :]
+            d_gelu = dot_nn(dy_buf[block, :], w_all[down])
+            made, slope = gelu_pair(hidden)
+            act[down, block, :] = made.astype(LOW)
+            act[up, block, :] = (d_gelu * slope).astype(LOW)
+        return run
+
+    slot = 28
+    for part in range(4):
+        if part == 3:
+            loop(RS_START + 20 + 2 - slot, lambda i: None, slot)
+            slot = RS_START + 20 + 2
+        loop(2, feed(part), slot)
+        loop(2, lambda i, part=part: feed(part)(i + 2))
+        slot += 2
+        gradient(4 + 2 * part, 4 + 2 * part, x_buf)()
+        service(slot)
+        gradient(5 + 2 * part, 5 + 2 * part, dy_buf)()
+        service(slot + 1)
+        slot += 2
+
+    def finish(i):
+        block, columns = at(i // 4, 512), at(i % 4, 512)
+
+        def total(pieces):
+            return sum(dot_nt(act[piece, block, :], w_all[piece, columns, :]) for piece in pieces)
+
+        x_buf[block, columns] = total((3, 5, 7, 9, 11)).astype(LOW)
+        first = total((0, 1, 2)) * rows[0:1, columns]
+        dy_buf[block, columns] = (first + total((4, 6, 8, 10)) * rows[2:3, columns]).astype(LOW)
+
+    last = RS_START + AG_SLOTS + 2
+    loop(16, finish)
+    loop(last - slot, lambda i: None, slot)
+    ends = [
+        pltpu.make_async_copy(x_buf, out_out, load_sem.at[0]),
+        pltpu.make_async_copy(dy_buf, u_out, load_sem.at[1]),
+        pltpu.make_async_copy(small, small_out, load_sem.at[2]),
+        pltpu.make_async_copy(gb, gb_out, load_sem.at[3]),
+    ]
+    for end in ends:
+        end.start()
+    for end in ends:
+        end.wait()
+    for n in range(8, 12):
+        red_copy(n).wait()
+
+
+def standardise_rows(values):
+    middle = jnp.mean(values, -1, keepdims=True)
+    centred = values - middle
+    spread = jnp.mean(centred * centred, -1, keepdims=True)
+    return centred, lax.rsqrt(spread + EPS)
+
+
+def layer_call(*operands):
+    anywhere = pl.BlockSpec(memory_space=pltpu.HBM)
+    shape = jax.ShapeDtypeStruct
+    dma = pltpu.SemaphoreType.DMA
+    return pl.pallas_call(
+        layer_kernel,
+        out_shape=(
+            shape((PIECES, ROWS, COLS), LOW),
+            shape((TOK, WIDTH), LOW),
+            shape((TOK, WIDTH), LOW),
+            shape((WIDTH, 128), WIDE),
+            shape((16, COLS), WIDE),
+        ),
+        in_specs=[anywhere] * len(operands),
+        out_specs=[anywhere] * 5,
+        scratch_shapes=[
+            pltpu.VMEM((PIECES, WIDTH, COLS), LOW),
+            pltpu.VMEM((PIECES, TOK, COLS), LOW),
+            pltpu.VMEM((TOK, WIDTH), LOW),
+            pltpu.VMEM((TOK, WIDTH), LOW),
+            pltpu.VMEM((RING, WIDTH, COLS), LOW),
+            pltpu.VMEM((2, 4, HOPS, ROWS, COLS), LOW),
+            pltpu.VMEM((4, ROWS, COLS), LOW),
+            pltpu.VMEM((WIDTH, 128), WIDE),
+            pltpu.VMEM((16, COLS), WIDE),
+            pltpu.VMEM((LENGTH, COLS), WIDE),
+            pltpu.VMEM((LENGTH, COLS), WIDE),
+            pltpu.VMEM((TOK, 128), WIDE),
+            pltpu.VMEM((8, LENGTH), WIDE),
+            pltpu.VMEM((8, WIDTH), WIDE),
+            pltpu.VMEM((8, COLS), WIDE),
+            dma((7,)),
+            dma((PIECES,)),
+            dma((2, PIECES, HOPS)),
+            dma((2, PIECES, HOPS)),
+            dma((2, PIECES, HOPS)),
+            dma((2, PIECES, HOPS)),
+            dma((PIECES,)),
+        ],
+        compiler_params=pltpu.CompilerParams(collective_id=0, has_side_effects=True, vmem_limit_bytes=64000 * 1024),
+    )(*operands)
+
+
+def fused_body(tokens, block_place, w_qkv, b_qkv, w_o_t, b_o, w_up, b_up, w_down_t, b_down,
+               norm1_gain, norm1_shift, norm2_gain, norm2_shift, cotangent):
+    place = lax.axis_index("seq") * 4 + lax.axis_index("ctx")
+    both = lax.all_gather(jnp.stack([tokens[0], cotangent[0]]), PLANE, axis=0, tiled=False)
+    x_all, dy_all = both[:, 0].reshape(TOK, WIDTH), both[:, 1].reshape(TOK, WIDTH)
+    places = lax.all_gather(block_place[0], "seq", axis=0, tiled=False)
+    small = (b_qkv, b_o, b_up, b_down, norm1_gain, norm1_shift, norm2_gain, norm2_shift)
+    packed = lax.all_gather(jnp.concatenate(small), "fsdp", axis=0, tiled=False)
+    unpacked, start = [], 0
+    for part in small:
+        size = part.shape[0]
+        unpacked.append(packed[:, start : start + size].reshape(-1).astype(WIDE))
+        start += size
+    bias_qkv, bias_o, bias_up, bias_down, gain1, shift1, gain2, shift2 = unpacked
+
+    positions = (places[:, :, None] * BLK + jnp.arange(BLK, dtype=jnp.int32)).reshape(2, LENGTH)
+    cosine, sine = angles(positions.reshape(-1))
+    flat = positions.astype(WIDE).reshape(TOK, 1)
+    table = jnp.concatenate([cosine, sine, jnp.broadcast_to(flat, (TOK, 64))], 1)
+    pos_row = jnp.concatenate([positions.astype(WIDE), jnp.zeros((6, LENGTH), WIDE)])
+    rows = jnp.concatenate([jnp.stack([gain1, shift1, gain2, shift2]), jnp.zeros((4, WIDTH), WIDE)])
+    own_qkv = lax.dynamic_slice(bias_qkv.reshape(3, WIDTH), (0, place * COLS), (3, COLS))
+    own_up = lax.dynamic_slice(bias_up, (place * 1024,), (1024,)).reshape(4, COLS)
+    bias = jnp.concatenate([own_qkv, own_up, jnp.zeros((1, COLS), WIDE)])
+    cols = jnp.concatenate([shift1[:, None], shift2[:, None], jnp.zeros((WIDTH, 126), WIDE)], 1)
+
+    red, out_part, u_part, norms, gb = layer_call(
+        x_all, dy_all, w_qkv, w_o_t, w_up, w_down_t, table, pos_row, rows, bias, cols)
+
+    x_own, dy_own = tokens[0].astype(WIDE), cotangent[0].astype(WIDE)
+    out_sum = lax.psum_scatter(out_part, PLANE, scatter_dimension=0, tiled=True).astype(WIDE)
+    u_sum = lax.psum_scatter(u_part, PLANE, scatter_dimension=0, tiled=True).astype(WIDE)
+    output = (x_own + out_sum + bias_o + bias_down).astype(LOW)[None]
+    hat_own, scale_own = standardise(x_own)
+    d_x = scale_own * (u_sum - jnp.mean(u_sum, -1, keepdims=True) - hat_own * jnp.mean(u_sum * hat_own, -1, keepdims=True))
+    input_grad = (dy_own + d_x).astype(LOW)[None]
+
+    gathered = lax.all_gather(red, PLANE, axis=0, tiled=False)
+    g_qkv = gathered[:, :3].transpose(2, 1, 0, 3).reshape(ROWS, 3 * WIDTH).astype(WIDE)
+    g_o = gathered[:, 3].transpose(1, 0, 2).reshape(ROWS, WIDTH).astype(WIDE)
+    g_up = gathered[:, 4::2].transpose(2, 0, 1, 3).reshape(ROWS, 4 * WIDTH).astype(WIDE)
+    g_down = gathered[:, 5::2].transpose(2, 0, 1, 3).reshape(ROWS, 4 * WIDTH).astype(WIDE)
+
+    full_qkv = lax.dynamic_update_slice(jnp.zeros((3, WIDTH), WIDE), gb[:3], (0, place * COLS)).reshape(-1)
+    full_up = lax.dynamic_update_slice(jnp.zeros((4 * WIDTH,), WIDE), gb[4:12:2].reshape(-1), (place * 1024,))
+    sums = lax.psum((full_qkv, jnp.sum(dy_own, 0), full_up, norms[:, 8] / gain1, norms[:, 9], norms[:, 10] / gain2, norms[:, 11]), PLANE + ("fsdp",))
+    mine = lax.axis_index("fsdp")
+    sums = [lax.dynamic_slice_in_dim(s, mine * (s.shape[0] // 4), s.shape[0] // 4, 0) for s in sums]
+    return (output, input_grad, g_qkv, sums[0], g_o, sums[1], g_up, sums[2], g_down, sums[1], sums[3], sums[4], sums[5], sums[6])
+
+
 def solution(mesh):
     tok = P(("seq", "fsdp"), "ctx", None)
     mat, vec = P("fsdp", None), P("fsdp")
     params = (mat, vec, mat, vec, mat, vec, mat, vec, vec, vec, vec, vec)
     in_specs = (tok, P(("seq", "fsdp"), None)) + params + (tok,)
-    return jax.shard_map(body, mesh=mesh, in_specs=in_specs, out_specs=(tok, tok) + params, check_vma=False)
+    return jax.shard_map(fused_body if fits(mesh) else body, mesh=mesh, in_specs=in_specs, out_specs=(tok, tok) + params, check_vma=False)

time: 1340 us -> 1060 us (0.79)
  Pallas kernels: 0 us -> 375 us
  waiting for transfers between devices: 794 us -> 451 us
  matrix products: 206 us -> 0 us
  local copies, waits for them, and re-layouts: 208 us -> 153 us
  other arithmetic: 89.7 us -> 46.5 us
    pallas_call x0 -> x1, Pallas kernels: none -> 375 us  [layer_call(): pl.pallas_call(layer_kernel, out_shape=(shape((PIECES, ROWS, COLS), LOW),...]
    dot_general x17 -> x0, matrix products: 199 us -> none  [the longest x4 55.1 us: dot_nt(): lax.dot_general(left, right, (((1,), (1,)), ((), ())), preferred_element_...]
    all_gather x3 -> x2, waiting for transfers between devices: 369 us -> 186 us  [the longest x1 123 us: fused_body(): gathered = lax.all_gather(red, PLANE, axis=0, tiled=False)]
    reduce_scatter x3 -> x2, waiting for transfers between devices: 294 us -> 139 us  [the longest x1 72.7 us: fused_body(): lax.psum_scatter(out_part, PLANE, scatter_dimension=0, tiled=True)]
    unnamed x122 -> x52, local copies, waits for them, and re-layouts: 115 us -> 20.4 us
    convert_element_type x5 -> x7, local copies, waits for them, and re-layouts: 36.1 us -> 102 us  [the longest x2 41.6 us: fused_body(): gathered[:, 4::2].transpose(2, 0, 1, 3).reshape(ROWS, 4 * WIDTH)]
    concatenate x4 -> x2, other arithmetic: 29.2 us -> 2.91 us  [the longest x1 2.24 us: fused_body(): jnp.concatenate([cosine, sine, jnp.broadcast_to(flat, (TOK, 64))], 1)]
    reshape x6 -> x2, local copies, waits for them, and re-layouts: 17.2 us -> 0.64 us  [the longest x1 0.63 us: fused_body(): lax.dynamic_update_slice(jnp.zeros((3, WIDTH), WIDE), gb[:3], (0, place *...]
  transfers between devices with their start and end apart: 7 -> 5, of which waited for: 7 -> 5; matrix products, arithmetic and copies ran while one was open for 9% -> 3% of each run, Pallas kernels for 0% -> 0%
where the time goes in v2:
time: 1060 us; the launch traced here: 1050 us
  waiting for transfers between devices  451 us (43%)
  Pallas kernels  375 us (35%)
  local copies, waits for them, and re-layouts  153 us (14%)
  other arithmetic  46.5 us (4%)
  between operations  14.6 us (1%)
  blocking collectives  14 us (1%)
    pallas_call x1, Pallas kernels, layer_call(): pl.pallas_call(layer_kernel, out_shape=(shape((PIECES, ROWS, COLS), LOW),...  375 us
    psum x1, waiting for transfers between devices, fused_body(): lax.psum((full_qkv, jnp.sum(dy_own, 0), full_up, norms[:, 8] / gain1, nor...  123 us
    all_gather x1, waiting for transfers between devices, fused_body(): gathered = lax.all_gather(red, PLANE, axis=0, tiled=False)  123 us
    reduce_scatter x1, waiting for transfers between devices, fused_body(): lax.psum_scatter(out_part, PLANE, scatter_dimension=0, tiled=True)  72.7 us
    reduce_scatter x1, waiting for transfers between devices, fused_body(): lax.psum_scatter(u_part, PLANE, scatter_dimension=0, tiled=True)  66.8 us
    all_gather x1, waiting for transfers between devices, fused_body(): lax.all_gather(jnp.stack([tokens[0], cotangent[0]]), PLANE, axis=0, tiled...  63.4 us
    convert_element_type x2, local copies, waits for them, and re-layouts, fused_body(): gathered[:, 4::2].transpose(2, 0, 1, 3).reshape(ROWS, 4 * WIDTH)  41.6 us
    convert_element_type x2, local copies, waits for them, and re-layouts, fused_body(): gathered[:, 5::2].transpose(2, 0, 1, 3).reshape(ROWS, 4 * WIDTH)  41.6 us
  transfers between devices with their start and end apart: 5, of which 5 were waited for; matrix products, arithmetic and copies ran while one was open for 3% of the time, Pallas kernels for 0%

profile of v2, /device:TPU:13, one launch (start us, length us, event | category | flops | bytes accessed | tf_op | source)
XLA Modules:
  0.0 1053.4 jit_solution(13760520125835931151)
XLA Ops:
  7.2 3.1 pad_maximum_fusion
  10.9 3.1 all-gather.3
  16.3 11.0 %all-gather.4 = bf16[4,1,6656]{2,1,0:T(2,128)(2,1)S(1)} all-gather(bf16[1,1,6656]{2,1,0:T(2,128)(2,1)S(1)} %reshape.238), channel_id=3, replica_groups=mesh['seq'=2,'ctx'=4,'fsdp'=4] {'fsdp'}, dimensions={0}, use_global_device_ids=true | all-gather | bytes 66560 | tf_op jit(solution)/shard_map/all_gather | solution.py:637
  27.9 1.4 copy.80
  31.5 3.7 multiply_cosine_fusion
  35.6 2.2 pad_maximum_fusion.1
  37.8 63.4 %all-gather.8.cloned.1.call-done = bf16[16,256,2048]{2,1,0:T(8,128)(2,1)} async-done(((bf16[2,256,2048]{2,1,0:T(8,128)(2,1)}), bf16[16,256,2048]{2,1,0:T(8,128)(2,1)}) %all-gather.8.cloned.1.call-update) | async-done | bytes 16777232 | tf_op jit(solution)/shard_map/all_gather | solution.py:633
  101.2 12.0 %fusion.19 = (bf16[8,1,256,2048]{3,2,1,0:T(8,128)(2,1)}, bf16[8,1,256,2048]{3,2,1,0:T(8,128)(2,1)}) fusion(bf16[8,2,256,2048]{3,2,1,0:T(8,128)(2,1)} %bitcast.146), kind=kLoop, calls=%fused_computation.68 | loop fusion | bytes 33554432 | tf_op jit(solution)/shard_map/slice | solution.py:634
  113.2 374.6 %shard_map.254 = (bf16[12,512,256]{2,1,0:T(8,128)(2,1)}, bf16[2048,2048]{1,0:T(8,128)(2,1)}, bf16[2048,2048]{1,0:T(8,128)(2,1)}, f32[2048,128]{1,0:T(8,128)}, f32[16,256]{1,0:T(8,128)}) custom-call(bf16[2048,2048]{1,0:T(8,128)(2,1)} %bitcast.142, bf16[2048,2048]{1,0:T(8,128)(2,1)} %bitcast.141, bf16[512,6144]{1,0:T(8,128)(2,1)} %w_qkv.1, ...), custom_call_target="tpu_custom_call" | custom-call | tf_op jit(solution)/shard_map/pallas_call | solution.py:591
  489.8 5.4 slice_reduce_fusion
  499.8 123.5 %all-reduce.4.cloned.1.call-done = (f32[6144]{0:T(1024)}, f32[2048]{0:T(1024)}, f32[8192]{0:T(1024)}, f32[2048]{0:T(1024)}, f32[2048]{0:T(1024)}, /*index=5*/f32[2048]{0:T(1024)}, f32[2048]{0:T(1024)}) async-done(((f32[6144]{0:T(1024)}, f32[2048]{0:T(1024)}, f32[8192]{0:T(1024)}, f32[2048]{0:T(1024)}, f32[2048]{0:T(1024)}, /*index=5*/f32[2048]{0:T(1024)}, f32[2048]{0:T(1024)}), (f32[6144]{0:T(1024)}, ...) | async-done | bytes 98320 | tf_op jit(solution)/shard_map/psum | solution.py:675
  624.1 1.3 dynamic_slice.32
  625.4 1.3 dynamic_slice.33
  626.7 1.3 dynamic_slice.34
  628.1 1.3 dynamic_slice.35
  629.4 1.4 dynamic_slice.29
  630.8 1.3 dynamic_slice.31
  632.1 66.8 %reduce-scatter.5.cloned.1.call-done = bf16[256,2048]{1,0:T(8,128)(2,1)} async-done(((bf16[2048,2048]{1,0:T(8,128)(2,1)}), bf16[256,2048]{1,0:T(8,128)(2,1)}) %reduce-scatter.5.cloned.1.call-update) | async-done | bytes 1048592 | tf_op jit(solution)/shard_map/reduce_scatter | solution.py:661
  698.8 1.9 convert_reduce_fusion
  700.8 72.7 %reduce-scatter.3.cloned.1.call-done = bf16[256,2048]{1,0:T(8,128)(2,1)} async-done(((bf16[2048,2048]{1,0:T(8,128)(2,1)}), bf16[256,2048]{1,0:T(8,128)(2,1)}) %reduce-scatter.3.cloned.1.call-update) | async-done | bytes 1048592 | tf_op jit(solution)/shard_map/reduce_scatter | solution.py:660
  773.4 4.1 fusion.15
  777.6 122.7 %all-gather.10.cloned.1.call-done = bf16[96,512,256]{2,1,0:T(8,128)(2,1)} async-done(((bf16[12,512,256]{2,1,0:T(8,128)(2,1)}), bf16[96,512,256]{2,1,0:T(8,128)(2,1)}) %all-gather.10.cloned.1.call-update) | async-done | bytes 25165840 | tf_op jit(solution)/shard_map/all_gather | solution.py:667
  900.3 2.0 convert_bitcast_fusion.3
  902.3 9.1 convert_bitcast_fusion.2
  911.3 16.9 %convert_bitcast_fusion = (f32[512,8,4,256]{3,0,2,1:T(8,128)}, f32[512,8,4,256]{3,0,2,1:T(8,128)}) fusion(bf16[8,12,512,256]{3,2,1,0:T(8,128)(2,1)} %bitcast.145), kind=kLoop, calls=%fused_computation | loop fusion | flops 8388608 | bytes 50331648 | tf_op jit(solution)/shard_map/convert_element_type | solution.py:671
  928.3 2.6 copy.71
  930.9 16.4 %copy.64 = f32[512,3,8,256]{3,2,1,0:T(8,128)} copy(f32[512,3,8,256]{3,0,1,2:T(8,128)} %convert_bitcast_fusion.2) | data formatting | bytes 25165824 | tf_op jit(solution)/shard_map/convert_element_type | solution.py:668
  947.3 15.4 %copy.85 = f32[64,8,24,256]{3,1,2,0:T(8,128)} copy(f32[64,8,24,256]{3,2,1,0:T(8,128)} %bitcast.140) | data formatting | bytes 25165824
  962.7 20.9 %copy.67 = f32[512,8,4,256]{3,2,1,0:T(4,128)} copy(f32[512,8,4,256]{3,0,2,1:T(8,128)} %get-tuple-element.37) | data formatting | bytes 33554432 | tf_op jit(solution)/shard_map/convert_element_type | solution.py:671
  983.6 20.6 %reshape.229 = f32[512,8192]{1,0:T(8,128)} reshape(f32[512,8,4,256]{3,2,1,0:T(4,128)} %copy.67) | data formatting | bytes 33554432 | tf_op jit(solution)/shard_map/convert_element_type | solution.py:671
  1004.3 20.9 %copy.66 = f32[512,8,4,256]{3,2,1,0:T(4,128)} copy(f32[512,8,4,256]{3,0,2,1:T(8,128)} %get-tuple-element.38) | data formatting | bytes 33554432 | tf_op jit(solution)/shard_map/convert_element_type | solution.py:670
  1025.2 20.6 %reshape.228 = f32[512,8192]{1,0:T(8,128)} reshape(f32[512,8,4,256]{3,2,1,0:T(4,128)} %copy.66) | data formatting | bytes 33554432 | tf_op jit(solution)/shard_map/convert_element_type | solution.py:670
  (98 shorter events, 13.9 us)
Async XLA Ops:
  7.2 94.0 %all-gather.8.cloned.1.call-start = ((), (), s32[]{:S(2)}) async-start(), calls=%async_computation.4 | async-start | bytes 18874368 | tf_op jit(solution)/shard_map/all_gather | solution.py:633
  10.3 0.7 copy-start.13
  10.3 3.9 copy-start.5
  10.3 4.1 copy-start.8
  10.3 4.3 copy-start.6
  10.3 4.3 copy-start.9
  10.3 4.6 copy-start.10
  10.3 4.8 copy-start.11
  10.3 5.0 copy-start.12
  10.3 5.2 copy-start.7
  10.4 19.6 %copy-start.1 = (bf16[1,256,2048]{2,1,0:T(8,128)(2,1)S(1)}, bf16[1,256,2048]{2,1,0:T(8,128)(2,1)}, u32[]{:S(2)}) copy-start(bf16[1,256,2048]{2,1,0:T(8,128)(2,1)} %param.29) | copy-start | bytes 3145732
  10.4 612.9 %all-reduce.4.cloned.1.call-start = ((), (), s32[]{:S(2)}) async-start(), calls=%async_computation.6 | async-start | bytes 196608 | tf_op jit(solution)/shard_map/psum | solution.py:675
  30.0 5.5 copy-start.2
  495.4 1.2 copy-start.3
  496.6 202.2 %reduce-scatter.5.cloned.1.call-start = ((), (), s32[]{:S(2)}) async-start(), calls=%async_computation.3 | async-start | bytes 9437184 | tf_op jit(solution)/shard_map/reduce_scatter | solution.py:661
  497.4 276.1 %reduce-scatter.3.cloned.1.call-start = ((), (), s32[]{:S(2)}) async-start(), calls=%async_computation.2 | async-start | bytes 9437184 | tf_op jit(solution)/shard_map/reduce_scatter | solution.py:660
  497.9 1.2 copy-start
  498.0 402.3 %all-gather.10.cloned.1.call-start = ((), (), s32[]{:S(2)}) async-start(), calls=%async_computation.5 | async-start | bytes 28311552 | tf_op jit(solution)/shard_map/all_gather | solution.py:667
  624.1 421.8 %copy-start.4 = (f32[512]{0:T(512)}, f32[512]{0:T(512)S(1)}, u32[]{:S(2)}) copy-start(f32[512]{0:T(512)S(1)} %dynamic_slice.30) | copy-start | bytes 6148
Sparse Core Ops, SparseCore 0:
  10.5 90.6 all-gather.7
  496.7 126.5 all-reduce.3
  627.2 71.6 reduce-scatter.4
  702.1 71.2 reduce-scatter.2
  775.3 124.9 all-gather.9

commit v3 on v1

--- a/solution.py
+++ b/solution.py
@@ -3,6 +3,8 @@
 import jax
 import jax.numpy as jnp
 from jax import lax
+from jax.experimental import pallas as pl
+from jax.experimental.pallas import tpu as pltpu
 from jax.sharding import PartitionSpec as P
 
 HEADS = 8
@@ -223,9 +225,862 @@
     )
 
 
+MESH = pl.DeviceIdType.MESH
+PIECES = 12
+ROWS = 512
+COLS = 256
+WIDTH = 2048
+TOK = 2048
+OWN = 256
+LENGTH = 1024
+HOPS = 3
+SLOTS = 36
+RS_START = 18
+RING = 6
+LAST = RS_START + SLOTS + 7
+SCALING = 1.0 / math.sqrt(HEAD)
+
+
+def fits(mesh):
+    return dict(mesh.shape) == {"seq": 2, "ctx": 4, "fsdp": 4}
+
+
+def at(index, size):
+    return pl.ds(pl.multiple_of(index * size, size), size)
+
+
+def remote(source, target, sent, came, device):
+    return pltpu.make_async_remote_copy(
+        src_ref=source, dst_ref=target, send_sem=sent, recv_sem=came, device_id=device, device_id_type=MESH)
+
+
+def layer_kernel(tokens, cotangent, w_qkv, w_o, w_up, w_down, vec_own, place_own, turns,
+                 out, input_grad, small_out, gout, x_land, core_land, first_land, second_land,
+                 w_all, act, x_buf, dy_buf, g_ring, landing, small, gb, tab, pos, rows, bias,
+                 stage, vecs, vec32, places, pack, pack_z, pack_p, final,
+                 load_sem, own_sem, ag_send, ag_recv, rs_send, rs_recv, red_sem, ga_send, ga_recv,
+                 vec_send, vec_recv, pk_send, pk_recv, pp_send, pp_recv, core_send, core_recv, one_send, one_recv,
+                 two_send, two_recv):
+    y, c, z = lax.axis_index("seq"), lax.axis_index("ctx"), lax.axis_index("fsdp")
+    core = lax.rem(c, 2)
+    chip = c // 2
+    place = y * 4 + c
+    right, left = (y, c, jnp.minimum(z + 1, 3)), (y, c, jnp.maximum(z - 1, 0))
+    c_x, c_core = lax.rem(c + 2, 4), c + 1 - 2 * core
+    dev_x, dev_y, dev_c = (y, c_x, z), (1 - y, c, z), (y, c_core, z)
+    place_x, place_y, place_d = y * 4 + c_x, (1 - y) * 4 + c, (1 - y) * 4 + c_x
+    c_core_x = lax.rem(c_core + 2, 4)
+    place_c, place_cx, place_cy, place_cd = y * 4 + c_core, y * 4 + c_core_x, (1 - y) * 4 + c_core, (1 - y) * 4 + c_core_x
+    above = [(y, c, lax.rem(z + d, 4)) for d in (1, 2, 3)]
+    beside = []
+    for d in range(1, 8):
+        other = lax.rem(place + d, 8)
+        beside.append((other // 4, lax.rem(other, 4), z))
+    lane = lax.broadcasted_iota(jnp.int32, (1, 128), 1)
+
+    barrier = pltpu.get_barrier_semaphore()
+    for device in above + beside:
+        pl.semaphore_signal(barrier, inc=1, device_id=device, device_id_type=MESH)
+
+    def own_piece(i):
+        if i < 3:
+            source = w_qkv.at[:, at(i * 8 + place, COLS)]
+        elif i == 3:
+            source = w_o.at[:, at(place, COLS)]
+        else:
+            source = (w_up if i % 2 == 0 else w_down).at[:, at(place * 4 + (i - 4) // 2, COLS)]
+        return pltpu.make_async_copy(source, w_all.at[i, at(z, ROWS)], own_sem.at[i])
+
+    loads = [
+        pltpu.make_async_copy(tokens.at[0], x_land.at[place], load_sem.at[0]),
+        pltpu.make_async_copy(cotangent.at[0], dy_buf.at[at(place, OWN)], load_sem.at[1]),
+        pltpu.make_async_copy(vec_own, vecs.at[z], load_sem.at[2]),
+        pltpu.make_async_copy(place_own, places.at[y], load_sem.at[3]),
+        pltpu.make_async_copy(turns, small.at[pl.ds(0, LENGTH)], load_sem.at[4]),
+    ]
+    for i in range(PIECES):
+        own_piece(i).start()
+    for load in loads:
+        load.start()
+    pl.semaphore_wait(barrier, 10)
+
+    def gather(tag, source, target):
+        def copy(k):
+            sent, came = ga_send.at[tag, k], ga_recv.at[tag, k]
+            if k == 0:
+                return remote(source(0), target(place, 0), sent, came, dev_x)
+            if k == 1:
+                return remote(source(1), target(place, 1), sent, came, dev_x)
+            if k == 2:
+                return remote(source(1), target(place, 1), sent, came, dev_y)
+            if k == 3:
+                return remote(source(0), target(place, 0), sent, came, dev_y)
+            if k == 4:
+                return remote(source(None), target(place, None), sent, came, dev_c)
+            if k == 5:
+                return remote(target(place_x, 0), target(place_x, 0), sent, came, dev_y)
+            if k == 6:
+                return remote(target(place_y, 1), target(place_y, 1), sent, came, dev_x)
+            which = (place_x, place_y, place_d)[k - 7]
+            return remote(target(which, None), target(which, None), sent, came, dev_c)
+
+        def arrived(k):
+            spot = (
+                (place_x, 0), (place_x, 1), (place_y, 1), (place_y, 0), (place_c, None),
+                (place_d, 0), (place_d, 1), (place_cx, None), (place_cy, None), (place_cd, None),
+            )[k]
+            here = target(*spot)
+            remote(here, here, ga_send.at[tag, k], ga_recv.at[tag, k], dev_c).wait_recv()
+
+        def start():
+            for k in (0, 2, 1, 3, 4):
+                copy(k).start()
+
+        def middle():
+            arrived(0)
+            copy(5).start()
+            arrived(2)
+            copy(6).start()
+
+        def forward():
+            arrived(1)
+            copy(7).start()
+            arrived(3)
+            copy(8).start()
+
+        def far():
+            arrived(5)
+            arrived(6)
+            copy(9).start()
+
+        def end():
+            for k in (4, 7, 8, 9):
+                arrived(k)
+            for k in range(10):
+                copy(k).wait_send()
+
+        return start, middle, forward, far, end
+
+    def half_of(ref, half, size):
+        return ref if half is None else ref.at[pl.ds(half * size, size)]
+
+    x_gather = gather(0, lambda half: half_of(tokens.at[0], half, 128), lambda who, half: half_of(x_land.at[who], half, 128))
+    dy_gather = gather(
+        1, lambda half: half_of(cotangent.at[0], half, 128),
+        lambda who, half: dy_buf.at[at(who, OWN)] if half is None else dy_buf.at[at(who * 2 + half, 128)])
+    x_gather[0]()
+
+    def vec_copy(d):
+        return remote(vec_own, vecs.at[z], vec_send.at[d], vec_recv.at[d], above[d])
+
+    def place_copy():
+        return remote(place_own, places.at[y], vec_send.at[3], vec_recv.at[3], dev_y)
+
+    for d in range(3):
+        vec_copy(d).start()
+    place_copy().start()
+    for i in range(PIECES):
+        own_piece(i).wait()
+
+    def parts(s):
+        return (s // 6) * 2 + s % 2, (s // 2) % 3
+
+    def ag_copy(way, piece, hop, shard):
+        block = w_all.at[piece, at(shard, ROWS)]
+        return remote(block, block, ag_send.at[way, piece, hop], ag_recv.at[way, piece, hop], right if way == 0 else left)
+
+    def ag_service(slot):
+        before = slot - 2
+        old, old_hop = parts(jnp.maximum(before, 0))
+        live = (before >= 0) & (before < SLOTS)
+
+        @pl.when(live & (z >= 1) & (z - 1 - old_hop >= 0))
+        def _():
+            ag_copy(0, old, old_hop, z - 1 - old_hop).wait_recv()
+
+        @pl.when(live & (z <= 2) & (z + 1 + old_hop <= 3))
+        def _():
+            ag_copy(1, old, old_hop, z + 1 + old_hop).wait_recv()
+
+        piece, hop = parts(jnp.minimum(slot, SLOTS - 1))
+
+        @pl.when((slot < SLOTS) & (z <= 2) & (z - hop >= 0))
+        def _():
+            ag_copy(0, piece, hop, z - hop).start()
+
+        @pl.when((slot < SLOTS) & (z >= 1) & (z + hop <= 3))
+        def _():
+            ag_copy(1, piece, hop, z + hop).start()
+
+        @pl.when(live & (z <= 2) & (z - old_hop >= 0))
+        def _():
+            ag_copy(0, old, old_hop, z - old_hop).wait_send()
+
+        @pl.when(live & (z >= 1) & (z + old_hop <= 3))
+        def _():
+            ag_copy(1, old, old_hop, z + old_hop).wait_send()
+
+    def rs_piece(n):
+        return jnp.where(n < 4, 3 - n, 4 + (n - 4) // 2 + 4 * (n % 2))
+
+    def landing_slot(n, hop):
+        return jnp.where(hop < 2, (n % 2) * 2 + hop, 4 + n % 4)
+
+    def rs_copy(way, n, hop, shard):
+        return remote(
+            g_ring.at[n % RING, at(shard, ROWS)], landing.at[way, landing_slot(n, hop)],
+            rs_send.at[way, n, hop], rs_recv.at[way, n, hop], right if way == 0 else left)
+
+    def rs_add(way, n, hop, shard):
+        rs_copy(way, n, hop, shard).wait_recv()
+        block = g_ring.at[n % RING, at(shard, ROWS)]
+        block[...] = (block[...].astype(WIDE) + landing[way, landing_slot(n, hop)].astype(WIDE)).astype(LOW)
+
+    def red_copy(n):
+        return pltpu.make_async_copy(g_ring.at[n % RING, at(z, ROWS)], gout.at[rs_piece(n), place], red_sem.at[n])
+
+    def red_gather(n):
+        piece = rs_piece(n)
+        return gather(
+            2 + n, lambda half: half_of(gout.at[piece, place], half, 256),
+            lambda who, half: half_of(gout.at[piece, who], half, 256))
+
+    def rs_service(slot):
+        before = slot - 2
+        old, old_hop = parts(jnp.clip(before, 0, SLOTS - 1))
+        live = (before >= 0) & (before < SLOTS)
+
+        @pl.when(live & (z >= 1) & (z - 1 <= old_hop))
+        def _():
+            rs_add(0, old, old_hop, z + 2 - old_hop)
+
+        @pl.when(live & (z <= 2) & (2 - z <= old_hop))
+        def _():
+            rs_add(1, old, old_hop, z - 2 + old_hop)
+
+        piece, hop = parts(jnp.clip(slot, 0, SLOTS - 1))
+        sending = (slot >= 0) & (slot < SLOTS)
+
+        @pl.when(sending & (z <= 2) & (z <= hop))
+        def _():
+            rs_copy(0, piece, hop, z + 3 - hop).start()
+
+        @pl.when(sending & (z >= 1) & (3 - z <= hop))
+        def _():
+            rs_copy(1, piece, hop, z - 3 + hop).start()
+
+        @pl.when(live & (z <= 2) & (z <= old_hop))
+        def _():
+            rs_copy(0, old, old_hop, z + 3 - old_hop).wait_send()
+
+        @pl.when(live & (z >= 1) & (3 - z <= old_hop))
+        def _():
+            rs_copy(1, old, old_hop, z - 3 + old_hop).wait_send()
+
+        @pl.when(live & (old_hop == 2))
+        def _():
+            red_copy(old).start()
+            red_copy(old).wait()
+            red_gather(old)[0]()
+
+        for step, delay in ((1, 1), (2, 2), (3, 3), (4, 5)):
+            begun = slot - delay
+            n = jnp.clip((begun // 6) * 2 - 2 + begun % 6, 0, PIECES - 1)
+
+            @pl.when((begun >= 6) & (begun < SLOTS + 6) & (begun % 6 < 2))
+            def _(step=step, n=n):
+                red_gather(n)[step]()
+
+    def service(slot):
+        if isinstance(slot, int):
+            if slot < SLOTS + 2:
+                ag_service(jnp.int32(slot))
+            if slot >= RS_START:
+                rs_service(jnp.int32(slot - RS_START))
+        else:
+            ag_service(slot)
+            rs_service(slot - RS_START)
+
+    def services(first, last, early=False):
+        def step(slot, carry):
+            ag_service(slot)
+            if not early:
+                rs_service(slot - RS_START)
+            return carry
+
+        lax.fori_loop(first, last, step, 0)
+
+    def loop(count, body, first=None, ag=True, rs=True):
+        def step(i, carry):
+            if first is not None:
+                if ag:
+                    ag_service(first + i)
+                if rs:
+                    rs_service(first + i - RS_START)
+            body(i)
+            return carry
+
+        lax.fori_loop(0, count, step, 0)
+
+    services(0, 2, True)
+    for load in loads[2:]:
+        load.wait()
+    for d in range(3):
+        here = vecs.at[lax.rem(z + 3 - d, 4)]
+        remote(here, here, vec_send.at[d], vec_recv.at[d], above[d]).wait_recv()
+    other = places.at[1 - y]
+    remote(other, other, vec_send.at[3], vec_recv.at[3], dev_y).wait_recv()
+    for shard in range(4):
+        vec32[pl.ds(shard * 16, 16), :] = vecs[shard].astype(WIDE)
+        for k in range(4):
+            rows[k : k + 1, pl.ds(shard * ROWS, ROWS)] = vec32[shard * 16 + 9 + k : shard * 16 + 10 + k, :]
+        rows[4:5, pl.ds(shard * ROWS, ROWS)] = vec32[shard * 16 + 3 : shard * 16 + 4, :] + vec32[shard * 16 + 8 : shard * 16 + 9, :]
+        rows[5:8, pl.ds(shard * ROWS, ROWS)] = jnp.zeros((3, ROWS), WIDE)
+    for kind in range(3):
+        flat = kind * WIDTH + place * COLS
+        bias[kind : kind + 1, :] = vec32[pl.ds((flat // 1536) * 16 + (flat % 1536) // 512, 1), at((flat % 512) // 256, COLS)]
+    for part in range(4):
+        flat = place * 1024 + part * COLS
+        bias[3 + part : 4 + part, :] = vec32[pl.ds((flat // 2048) * 16 + 4 + (flat % 2048) // 512, 1), at((flat % 512) // 256, COLS)]
+    def set_place(i, carry):
+        seq, block = i // 8, i % 8
+        value = jnp.sum(jnp.where(lane == block, places[seq, 0:1, :], 0.0), 1, keepdims=True)
+        made = jnp.zeros((BLK, 128), WIDE)
+        for b in range(8):
+            made = jnp.where(value == float(b), small[pl.ds(b * BLK, BLK), :], made)
+        tab[at(i, BLK), :] = made
+        pos[seq, :, at(block, BLK)] = jnp.broadcast_to(value * float(BLK) + lane.astype(WIDE), (8, BLK))
+        return carry
+
+    services(2, 3, True)
+    lax.fori_loop(0, 16, set_place, 0)
+    for shard in range(4):
+        tall = jnp.concatenate([rows[:, pl.ds(shard * ROWS, ROWS)], jnp.zeros((120, ROWS), WIDE)], 0)
+        small[pl.ds(shard * ROWS, ROWS), :] = jnp.transpose(tall)
+    x_gather[1]()
+    services(3, 5, True)
+    x_gather[2]()
+    dy_gather[0]()
+    services(5, 7, True)
+    x_gather[3]()
+    services(7, 8, True)
+    x_gather[4]()
+    loads[0].wait()
+
+    def norm_tile(which):
+        def run(i):
+            def part(n, carry):
+                block = at(i * 4 + n, 64)
+                centred, scale = standardise_rows(x_buf[block, :].astype(WIDE))
+                x_buf[block, :] = (centred * scale * rows[2 * which : 2 * which + 1, :] + rows[2 * which + 1 : 2 * which + 2, :]).astype(LOW)
+                return carry
+
+            lax.fori_loop(0, 4, part, 0)
+        return run
+
+    def load_x():
+        copies = [pltpu.make_async_copy(x_land.at[p], x_buf.at[pl.ds(p * OWN, OWN)], own_sem.at[p]) for p in range(8)]
+        for copy in copies:
+            copy.start()
+        for copy in copies:
+            copy.wait()
+
+    def norm(which, first, rs):
+        load_x()
+
+        def body(i):
+            for n in range(4):
+                norm_tile(which)(4 * i + n)
+
+        loop(2, body, first, rs=rs)
+
+    norm(0, 8, False)
+    dy_gather[1]()
+
+    def turned(values, block, sign):
+        entry = tab[block, :]
+        cosine = jnp.where(lane < 32, entry, jnp.where(lane < 64, pltpu.roll(entry, 32, 1), 1.0))
+        sine = jnp.where(lane < 32, -pltpu.roll(entry, 96, 1), jnp.where(lane < 64, entry, 0.0))
+        low = values[:, :128]
+        partner = jnp.where(lane < 32, pltpu.roll(low, 96, 1), pltpu.roll(low, 32, 1))
+        return jnp.concatenate([low * cosine + partner * (sine * sign), values[:, 128:]], 1)
+
+    def project(kind):
+        def run(i):
+            block = at(i, 512)
+            made = dot_nn(x_buf[block, :], w_all[kind]) + bias[kind : kind + 1, :]
+            if kind < 2:
+                made = turned(made, block, 1.0)
+            act[9 + kind, block, :] = made.astype(LOW)
+        return run
+
+    services(10, 11, True)
+    loop(4, project(0))
+    dy_gather[2]()
+    services(11, 12, True)
+    loop(4, project(1))
+    services(12, 14, True)
+    loop(4, project(2))
+    dy_gather[3]()
+    dy_gather[4]()
+    loads[1].wait()
+
+    def attend(i):
+        seq = i // 4
+        block, keys = at(i, 256), at(seq, LENGTH)
+
+        q, k, v = act[9, block, :], act[10, keys, :], act[11, keys, :]
+        kept = tab[block, 64:65] >= pos[seq, 0:1, :]
+        scores = jnp.where(kept, dot_nt(q, k) * SCALING, -1e30)
+        expo = jnp.exp(scores - jnp.max(scores, -1, keepdims=True))
+        p = expo * (1.0 / jnp.sum(expo, -1, keepdims=True))
+        p_low = p.astype(LOW)
+        act[3, block, :] = dot_nn(p_low, v).astype(LOW)
+        d_attn = dot_nn(dy_buf[block, :], w_all[3]).astype(LOW)
+        dp = dot_nt(d_attn, v)
+        ds = jnp.where(kept, p * (dp - jnp.sum(p * dp, -1, keepdims=True)), 0.0).astype(LOW)
+        act[0, block, :] = turned(dot_nn(ds, k) * SCALING, block, -1.0).astype(LOW)
+        act[8, block, :] = d_attn
+        for n in range(4):
+            g_ring[n, at(i % 4, 256), :] = ds[:, n * COLS : (n + 1) * COLS]
+            g_ring[n, at(4 + i % 4, 256), :] = p_low[:, n * COLS : (n + 1) * COLS]
+
+        @pl.when(i % 4 == 3)
+        def _():
+            def keyed(n, carry):
+                mine = at(seq * 4 + n, COLS)
+                d_keys = dot_tn(g_ring[n, 0:LENGTH, :], act[9, keys, :]) * SCALING
+                act[1, mine, :] = turned(d_keys, mine, -1.0).astype(LOW)
+                act[2, mine, :] = dot_tn(g_ring[n, LENGTH:, :], act[8, keys, :]).astype(LOW)
+                return carry
+
+            lax.fori_loop(0, 4, keyed, 0)
+
+    def attend_two(i):
+        def inner(n, carry):
+            attend(2 * i + n)
+            return carry
+
+        lax.fori_loop(0, 2, inner, 0)
+
+    loop(4, attend_two, 14, rs=False)
+
+    def gradient(piece, n, source):
+        summed = piece < 3 or (piece != 3 and piece % 2 == 0)
+        if summed:
+            gb[piece : piece + 1, :] = jnp.zeros((1, COLS), WIDE)
+
+            def count(i, carry):
+                gb[piece : piece + 1, :] += jnp.sum(act[piece, at(i, 256), :].astype(WIDE), 0, keepdims=True)
+                return carry
+
+            lax.fori_loop(0, 8, count, 0)
+
+        def part(s, carry):
+            block = at(s, ROWS)
+            made = dot_tn(source[:, block], act[piece])
+            g_ring[n % RING, block, :] = made.astype(LOW)
+            if summed:
+                mine = 0 if piece < 3 else 1
+                weight = w_all[piece, block, :].astype(WIDE)
+                sums = gb[piece : piece + 1, :]
+                gain = jnp.sum(weight * (made - small[block, 2 * mine + 1 : 2 * mine + 2] * sums), 1, keepdims=True)
+                shift = jnp.sum(weight * sums, 1, keepdims=True)
+                here = 8 + 2 * mine
+                old = small[block, :]
+                small[block, :] = old + jnp.where(lane == here, gain, 0.0) + jnp.where(lane == here + 1, shift, 0.0)
+            return carry
+
+        lax.fori_loop(0, 4, part, 0)
+
+    rows[5:6, :] = jnp.sum(dy_buf[at(place, OWN), :].astype(WIDE), 0, keepdims=True)
+    gradient(3, 0, dy_buf)
+    service(18)
+    gradient(2, 1, x_buf)
+    service(19)
+    gradient(1, 2, x_buf)
+    service(20)
+    gradient(0, 3, x_buf)
+    service(21)
+    norm(1, 22, True)
+
+    def feed(part):
+        up, down = 4 + 2 * part, 5 + 2 * part
+
+        def run(i):
+            for n in range(2):
+                block = at(2 * i + n, 512)
+                hidden = dot_nn(x_buf[block, :], w_all[up]) + bias[3 + part : 4 + part, :]
+                d_gelu = dot_nn(dy_buf[block, :], w_all[down])
+                made, slope = gelu_pair(hidden)
+                act[down, block, :] = made.astype(LOW)
+                act[up, block, :] = (d_gelu * slope).astype(LOW)
+        return run
+
+    slot = 24
+    for part in range(4):
+        if part == 3:
+            services(slot, SLOTS + 2)
+            slot = SLOTS + 2
+        loop(2, feed(part), slot)
+        slot += 2
+        gradient(4 + 2 * part, 4 + 2 * part, x_buf)
+        service(slot)
+        gradient(5 + 2 * part, 5 + 2 * part, dy_buf)
+        service(slot + 1)
+        slot += 2
+
+    for shard in range(4):
+        here = pl.ds(shard * ROWS, ROWS)
+        flat = jnp.transpose(small[here, :])
+        pack[shard, 0:1, :] = flat[8:9] / rows[0:1, here]
+        pack[shard, 1:2, :] = flat[9:10]
+        pack[shard, 2:3, :] = flat[10:11] / rows[2:3, here]
+        pack[shard, 3:4, :] = flat[11:12]
+        pack[shard, 4:5, :] = rows[5:6, here]
+        pack[shard, 5:8, :] = jnp.zeros((3, ROWS), WIDE)
+        pack[shard, 8:16, :] = jnp.zeros((8, ROWS), WIDE)
+        for kind in range(3):
+            pack[shard, 8 + kind : 9 + kind, :COLS] = gb[kind : kind + 1, :]
+        for part in range(4):
+            pack[shard, 11 + part : 12 + part, :COLS] = gb[4 + 2 * part : 5 + 2 * part, :]
+    pack_z[z] = pack[z]
+
+    def pack_copy(d):
+        return remote(pack.at[lax.rem(z + d + 1, 4)], pack_z.at[z], pk_send.at[d], pk_recv.at[d], above[d])
+
+    def peer_copy(d):
+        return remote(pack_p.at[place], pack_p.at[place], pp_send.at[d], pp_recv.at[d], beside[d])
+
+    for d in range(3):
+        pack_copy(d).start()
+
+    def sum_z():
+        for d in range(3):
+            here = pack_z.at[lax.rem(z + 3 - d, 4)]
+            remote(here, here, pk_send.at[d], pk_recv.at[d], above[d]).wait_recv()
+        pack_p[place] = pack_z[0] + pack_z[1] + pack_z[2] + pack_z[3]
+        for d in range(7):
+            peer_copy(d).start()
+
+    def sum_plane():
+        for d in range(7):
+            here = pack_p.at[lax.rem(place + 7 - d, 8)]
+            remote(here, here, pp_send.at[d], pp_recv.at[d], beside[d]).wait_recv()
+        total = pack_p[0, 0:8, :]
+        for p in range(1, 8):
+            total = total + pack_p[p, 0:8, :]
+        final[:, 0:ROWS] = total
+        final[:, ROWS:] = jnp.zeros((8, 2 * COLS), WIDE)
+        for r in range(6):
+            flat = 6 * z + r
+            final[r : r + 1, ROWS : ROWS + COLS] = pack_p[flat % 8, pl.ds(8 + flat // 8, 1), 0:COLS]
+        for r in range(8):
+            final[r : r + 1, ROWS + COLS :] = pack_p[2 * z + r // 4, 11 + r % 4 : 12 + r % 4, 0:COLS]
+
+    tiles = {"d": (1 - y) * 2 + 1 - chip, "x": y * 2 + 1 - chip, "y": (1 - y) * 2 + chip, "own": y * 2 + chip}
+    order = ("d", "x", "y", "own")
+    both = (x_buf, dy_buf)
+
+    def finish(tile):
+        def run(i):
+            block, columns = at(tile, 512), at(i, 512)
+
+            def total(pieces):
+                return sum(dot_nt(act[piece, block, :], w_all[piece, columns, :]) for piece in pieces)
+
+            x_buf[block, columns] = total((3, 5, 7, 9, 11)).astype(LOW)
+            first = total((0, 1, 2)) * rows[0:1, columns]
+            dy_buf[block, columns] = (first + total((4, 6, 8, 10)) * rows[2:3, columns]).astype(LOW)
+        return run
+
+    def block_of(name, whose):
+        return at(tiles[name] * 2 + whose, OWN)
+
+    def half_rows(name, half):
+        return at(tiles[name] * 4 + core * 2 + half, 128)
+
+    def core_copy(name, a):
+        i = order.index(name)
+        return remote(both[a].at[block_of(name, 1 - core)], core_land.at[i, a], core_send.at[i, a], core_recv.at[i, a], dev_c)
+
+    def first_copy(i, a):
+        name, half, device = (("d", 0, dev_x), ("d", 1, dev_y), ("x", 0, dev_x), ("y", 1, dev_y))[i]
+        return remote(both[a].at[half_rows(name, half)], first_land.at[i, a], one_send.at[i, a], one_recv.at[i, a], device)
+
+    def second_copy(i, a):
+        name, half, device = (("y", 0, dev_y), ("x", 1, dev_x))[i]
+        return remote(both[a].at[half_rows(name, half)], second_land.at[i, a], two_send.at[i, a], two_recv.at[i, a], device)
+
+    def fetch(source, a):
+        return pltpu.make_async_copy(source, stage.at[a], load_sem.at[a])
+
+    def add_in(copies, sources, spots):
+        for a in range(2):
+            copies[a].wait_recv()
+        for half, spot in enumerate(spots):
+            for a in range(2):
+                fetch(sources[a].at[pl.ds(half * 128, 128)], a).start()
+            for a in range(2):
+                fetch(sources[a].at[pl.ds(half * 128, 128)], a).wait()
+                both[a][spot, :] = (both[a][spot, :].astype(WIDE) + stage[a].astype(WIDE)).astype(LOW)
+
+    def core_start(name):
+        for a in range(2):
+            core_copy(name, a).start()
+
+    def core_add(name):
+        i = order.index(name)
+        add_in([core_copy(name, a) for a in range(2)], [core_land.at[i, a] for a in range(2)], [half_rows(name, 0), half_rows(name, 1)])
+
+    def first_start(i):
+        for a in range(2):
+            first_copy(i, a).start()
+
+    def first_add(i):
+        name, half = (("y", 0), ("x", 1), ("own", 0), ("own", 1))[i]
+        add_in([first_copy(i, a) for a in range(2)], [first_land.at[i, a] for a in range(2)], [half_rows(name, half)])
+
+    def second_start(i):
+        for a in range(2):
+            second_copy(i, a).start()
+
+    def second_add(i):
+        add_in([second_copy(i, a) for a in range(2)], [second_land.at[i, a] for a in range(2)], [half_rows("own", i)])
+
+    def finish_tile(name, first):
+        def body(i):
+            finish(tiles[name])(2 * i)
+            finish(tiles[name])(2 * i + 1)
+
+        loop(2, body, first, ag=False)
+        core_start(name)
+
+    finish_tile("d", 42)
+    finish_tile("x", 44)
+    core_add("d")
+    first_start(0)
+    first_start(1)
+    sum_z()
+    finish_tile("y", 46)
+    core_add("x")
+    first_start(2)
+    finish_tile("own", 48)
+    core_add("y")
+    first_start(3)
+    service(50)
+    service(51)
+    first_add(0)
+    second_start(0)
+    first_add(1)
+    second_start(1)
+    service(52)
+    core_add("own")
+    sum_plane()
+    service(53)
+    first_add(2)
+    service(54)
+    first_add(3)
+    service(55)
+    second_add(0)
+    service(56)
+    second_add(1)
+    service(57)
+
+    for half in range(2):
+        given = [tokens.at[0, pl.ds(half * 128, 128)], cotangent.at[0, pl.ds(half * 128, 128)]]
+        for a in range(2):
+            fetch(given[a], a).start()
+        for a in range(2):
+            fetch(given[a], a).wait()
+
+        def emit(i, carry, half=half):
+            here, mine = at(i, 64), at(place * 4 + half * 2 + i, 64)
+            inputs = stage[0, here, :].astype(WIDE)
+            x_buf[mine, :] = (inputs + x_buf[mine, :].astype(WIDE) + rows[4:5, :]).astype(LOW)
+            centred, scale = standardise_rows(inputs)
+            hat = centred * scale
+            u = dy_buf[mine, :].astype(WIDE)
+            inner = jnp.mean(u * hat, -1, keepdims=True)
+            d_x = scale * (u - jnp.mean(u, -1, keepdims=True) - hat * inner)
+            dy_buf[mine, :] = (stage[1, here, :].astype(WIDE) + d_x).astype(LOW)
+            return carry
+
+        lax.fori_loop(0, 2, emit, 0)
+    ends = [
+        pltpu.make_async_copy(x_buf.at[at(place, OWN)], out, load_sem.at[0]),
+        pltpu.make_async_copy(dy_buf.at[at(place, OWN)], input_grad, load_sem.at[1]),
+        pltpu.make_async_copy(final, small_out, load_sem.at[2]),
+    ]
+    for end in ends:
+        end.start()
+    services(58, LAST)
+    for end in ends:
+        end.wait()
+    for d in range(3):
+        vec_copy(d).wait_send()
+        pack_copy(d).wait_send()
+    place_copy().wait_send()
+    for d in range(7):
+        peer_copy(d).wait_send()
+    for a in range(2):
+        for name in order:
+            core_copy(name, a).wait_send()
+        for i in range(4):
+            first_copy(i, a).wait_send()
+        for i in range(2):
+            second_copy(i, a).wait_send()
+
+
+def standardise_rows(values):
+    middle = jnp.mean(values, -1, keepdims=True)
+    centred = values - middle
+    spread = jnp.mean(centred * centred, -1, keepdims=True)
+    return centred, lax.rsqrt(spread + EPS)
+
+
+def layer_call(*operands):
+    anywhere = pl.BlockSpec(memory_space=pltpu.HBM)
+    shape = jax.ShapeDtypeStruct
+    dma = pltpu.SemaphoreType.DMA
+    out_shape = (
+        shape((OWN, WIDTH), LOW),
+        shape((OWN, WIDTH), LOW),
+        shape((8, 1024), WIDE),
+        shape((PIECES, 8, ROWS, COLS), LOW),
+        shape((8, OWN, WIDTH), LOW),
+        shape((4, 2, OWN, WIDTH), LOW),
+        shape((4, 2, 128, WIDTH), LOW),
+        shape((2, 2, 128, WIDTH), LOW),
+    )
+    return pl.pallas_call(
+        layer_kernel,
+        out_shape=out_shape,
+        in_specs=[anywhere] * len(operands),
+        out_specs=[anywhere] * len(out_shape),
+        scratch_shapes=[
+            pltpu.VMEM((PIECES, WIDTH, COLS), LOW),
+            pltpu.VMEM((PIECES, TOK, COLS), LOW),
+            pltpu.VMEM((TOK, WIDTH), LOW),
+            pltpu.VMEM((TOK, WIDTH), LOW),
+            pltpu.VMEM((RING, WIDTH, COLS), LOW),
+            pltpu.VMEM((2, 8, ROWS, COLS), LOW),
+            pltpu.VMEM((WIDTH, 128), WIDE),
+            pltpu.VMEM((16, COLS), WIDE),
+            pltpu.VMEM((TOK, 128), WIDE),
+            pltpu.VMEM((2, 8, LENGTH), WIDE),
+            pltpu.VMEM((8, WIDTH), WIDE),
+            pltpu.VMEM((8, COLS), WIDE),
+            pltpu.VMEM((2, 128, WIDTH), LOW),
+            pltpu.VMEM((4, 16, ROWS), LOW),
+            pltpu.VMEM((64, ROWS), WIDE),
+            pltpu.VMEM((2, 8, 128), WIDE),
+            pltpu.VMEM((4, 16, ROWS), WIDE),
+            pltpu.VMEM((4, 16, ROWS), WIDE),
+            pltpu.VMEM((8, 16, ROWS), WIDE),
+            pltpu.VMEM((8, 1024), WIDE),
+            dma((5,)),
+            dma((PIECES,)),
+            dma((2, PIECES, HOPS)),
+            dma((2, PIECES, HOPS)),
+            dma((2, PIECES, HOPS)),
+            dma((2, PIECES, HOPS)),
+            dma((PIECES,)),
+            dma((2 + PIECES, 10)),
+            dma((2 + PIECES, 10)),
+            dma((4,)),
+            dma((4,)),
+            dma((3,)),
+            dma((3,)),
+            dma((7,)),
+            dma((7,)),
+            dma((4, 2)),
+            dma((4, 2)),
+            dma((4, 2)),
+            dma((4, 2)),
+            dma((2, 2)),
+            dma((2, 2)),
+        ],
+        compiler_params=pltpu.CompilerParams(collective_id=0, has_side_effects=True, vmem_limit_bytes=61 * 1024 * 1024),
+    )(*operands)
+
+
+def widen_kernel(first, second, g_qkv, g_o, g_up, g_down):
+    step = pl.program_id(0)
+
+    @pl.when(step < 3)
+    def _():
+        for p in range(8):
+            g_qkv[:, p * COLS : (p + 1) * COLS] = first[0, p].astype(WIDE)
+
+    @pl.when(step == 3)
+    def _():
+        for p in range(8):
+            g_o[:, p * COLS : (p + 1) * COLS] = first[0, p].astype(WIDE)
+
+    @pl.when((step >= 4) & (step < 12))
+    def _():
+        for part in range(4):
+            g_up[:, part * COLS : (part + 1) * COLS] = second[part, 0].astype(WIDE)
+
+    @pl.when(step >= 12)
+    def _():
+        for part in range(4):
+            g_down[:, part * COLS : (part + 1) * COLS] = second[part, 0].astype(WIDE)
+
+
+def widen(gathered):
+    shape = jax.ShapeDtypeStruct
+    return pl.pallas_call(
+        widen_kernel,
+        grid=(20,),
+        in_specs=[
+            pl.BlockSpec((1, 8, ROWS, COLS), lambda i: (jnp.minimum(i, 3), 0, 0, 0)),
+            pl.BlockSpec((4, 1, ROWS, COLS), lambda i: (jnp.where(i < 12, 1, 2), jnp.where(i < 4, 0, (i - 4) % 8), 0, 0)),
+        ],
+        out_specs=[
+            pl.BlockSpec((ROWS, WIDTH), lambda i: (0, jnp.minimum(i, 2))),
+            pl.BlockSpec((ROWS, WIDTH), lambda i: (0, 0)),
+            pl.BlockSpec((ROWS, 1024), lambda i: (0, jnp.clip(i - 4, 0, 7))),
+            pl.BlockSpec((ROWS, 1024), lambda i: (0, jnp.clip(i - 12, 0, 7))),
+        ],
+        out_shape=(shape((ROWS, 3 * WIDTH), WIDE), shape((ROWS, WIDTH), WIDE), shape((ROWS, 4 * WIDTH), WIDE), shape((ROWS, 4 * WIDTH), WIDE)),
+        compiler_params=pltpu.CompilerParams(vmem_limit_bytes=48 * 1024 * 1024),
+    )(gathered, gathered)
+
+
+def fused_body(tokens, block_place, w_qkv, b_qkv, w_o_t, b_o, w_up, b_up, w_down_t, b_down,
+               norm1_gain, norm1_shift, norm2_gain, norm2_shift, cotangent):
+    vec = jnp.concatenate([b_qkv, b_o, b_up, b_down, norm1_gain, norm1_shift, norm2_gain, norm2_shift, jnp.zeros((3 * ROWS,), LOW)])
+    place_own = jnp.broadcast_to(jnp.pad(block_place.astype(WIDE), ((0, 0), (0, 120))), (8, 128))
+    cosine, sine = angles(jnp.arange(LENGTH, dtype=jnp.int32))
+    where = jnp.broadcast_to(jnp.arange(LENGTH, dtype=WIDE)[:, None], (LENGTH, 64))
+    turns = jnp.concatenate([cosine, sine, where], 1)
+    results = layer_call(tokens, cotangent, w_qkv, w_o_t, w_up, w_down_t, vec.reshape(16, ROWS), place_own, turns)
+    output, input_grad, sums, gathered = results[:4]
+    g_qkv, g_o, g_up, g_down = widen(gathered)
+    grad_bias = sums[4, :ROWS]
+    return (
+        output[None],
+        input_grad[None],
+        g_qkv,
+        sums[:6, ROWS : ROWS + COLS].reshape(-1),
+        g_o,
+        grad_bias,
+        g_up,
+        sums[:, ROWS + COLS :].reshape(-1),
+        g_down,
+        grad_bias,
+        sums[0, :ROWS],
+        sums[1, :ROWS],
+        sums[2, :ROWS],
+        sums[3, :ROWS],
+    )
+
+
 def solution(mesh):
     tok = P(("seq", "fsdp"), "ctx", None)
     mat, vec = P("fsdp", None), P("fsdp")
     params = (mat, vec, mat, vec, mat, vec, mat, vec, vec, vec, vec, vec)
     in_specs = (tok, P(("seq", "fsdp"), None)) + params + (tok,)
-    return jax.shard_map(body, mesh=mesh, in_specs=in_specs, out_specs=(tok, tok) + params, check_vma=False)
+    return jax.shard_map(fused_body if fits(mesh) else body, mesh=mesh, in_specs=in_specs, out_specs=(tok, tok) + params, check_vma=False)

time: 1340 us -> 497 us (0.37)
  waiting for transfers between devices: 794 us -> 0 us
  Pallas kernels: 0 us -> 468 us
  matrix products: 206 us -> 0 us
  local copies, waits for them, and re-layouts: 208 us -> 14.9 us
  other arithmetic: 89.7 us -> 3.69 us
  blocking collectives: 14.8 us -> 0 us
  between operations: 15.1 us -> 1.12 us
    pallas_call x0 -> x2, Pallas kernels: none -> 468 us  [the longest x1 438 us: layer_call(): pl.pallas_call(layer_kernel, out_shape=out_shape, in_specs=[anywhere] * l...]
    all_gather x3 -> x0, waiting for transfers between devices: 369 us -> none  [the longest x1 186 us: body(): weights = lax.all_gather(own_cols, 'fsdp', axis=0, tiled=True)]
    reduce_scatter x3 -> x0, waiting for transfers between devices: 294 us -> none  [the longest x1 154 us: body(): reduced = lax.psum_scatter(grads, 'fsdp', scatter_dimension=0, tiled=True)]
    dot_general x17 -> x0, matrix products: 199 us -> none  [the longest x4 55.1 us: dot_nt(): lax.dot_general(left, right, (((1,), (1,)), ((), ())), preferred_element_...]
    psum x1 -> x0, waiting for transfers between devices: 132 us -> none  [body(): lax.psum((full_qkv, jnp.sum(dy_own, 0, dtype=WIDE), full_up, d_gain1, d_s...]
    unnamed x122 -> x19, local copies, waits for them, and re-layouts: 115 us -> 10.5 us
    convert_element_type x5 -> x0, local copies, waits for them, and re-layouts: 36.1 us -> none  [the longest x2 33.5 us: spread_hid(): return values.transpose(1, 0, 2).reshape(rows_own, hidden_all).astype(WIDE)]
    convert_element_type x3 -> x1, other arithmetic: 29 us -> 0.66 us  [fused_body(): block_place.astype(WIDE)]
  transfers between devices with their start and end apart: 7 -> 0, of which waited for: 7 -> 0; matrix products, arithmetic and copies ran while one was open for 9% -> 0% of each run, Pallas kernels for 0% -> 0%
where the time goes in v3:
time: 497 us; the launch traced here: 488 us
  Pallas kernels  468 us (94%)
  local copies, waits for them, and re-layouts  14.9 us (3%)
    pallas_call x1, Pallas kernels, layer_call(): pl.pallas_call(layer_kernel, out_shape=out_shape, in_specs=[anywhere] * l...  438 us
    pallas_call x1, Pallas kernels, widen(): pl.pallas_call(widen_kernel, grid=(20,), in_specs=[pl.BlockSpec((1, 8, RO...  30 us
    unnamed x19, local copies, waits for them, and re-layouts  10.5 us

profile of v3, /device:TPU:13, one launch (start us, length us, event | category | flops | bytes accessed | tf_op | source)
XLA Modules:
  0.0 488.1 jit_solution(6572117041180683143)
XLA Ops:
  0.6 0.7 convert_element_type.14
  1.3 0.6 broadcast_in_dim.26.place_own
  1.9 0.9 dynamic-update-slice
  2.8 0.9 dynamic-update-slice.1
  3.6 0.7 constant_dynamic-update-slice_fusion
  4.3 0.9 dynamic-update-slice.3
  5.2 0.9 dynamic-update-slice.4
  6.0 0.9 dynamic-update-slice.5
  6.9 0.9 dynamic-update-slice.6
  7.8 0.9 dynamic-update-slice.7
  8.6 0.3 dynamic-update-slice.8
  8.9 0.6 reshape.47.vec_own
  9.5 0.1 broadcast_in_dim.27
  9.6 1.9 multiply_cosine_fusion
  11.5 1.1 pad_maximum_fusion.turns
  12.7 438.4 %shard_map.254 = (bf16[256,2048]{1,0:T(8,128)(2,1)}, bf16[256,2048]{1,0:T(8,128)(2,1)}, f32[8,1024]{1,0:T(8,128)}, bf16[12,8,512,256]{3,2,1,0:T(8,128)(2,1)}, bf...) custom-call(bf16[1,256,2048]{2,1,0:T(8,128)(2,1)} %tokens.1, ...), custom_call_target="tpu_custom_call" | custom-call | tf_op jit(solution)/shard_map/pallas_call | solution.py:956
  451.0 0.7 slice_bitcast_fusion
  451.7 0.6 copy.30
  452.3 0.7 slice.21
  453.0 1.5 fusion
  454.5 0.0 copy-start.2
  454.5 0.6 reshape.48
  455.1 0.0 copy-start.1
  455.1 0.0 copy-start
  455.1 30.0 %shard_map.255 = (f32[512,6144]{1,0:T(8,128)}, f32[512,2048]{1,0:T(8,128)}, f32[512,8192]{1,0:T(8,128)}, f32[512,8192]{1,0:T(8,128)}) custom-call(bf16[12,8,512,256]{3,2,1,0:T(8,128)(2,1)} %get-tuple-element.24.first.second, bf16[12,8,512,256]{3,2,1,0:T(8,128)(2,1)} %get-tuple-element.24.first.second), custom_call_target="tpu_custom_call" | custom-call | tf_op jit(solution)/shard_map/pallas_call | solution.py:1034
  485.1 0.0 copy-done.2
  485.1 0.6 copy.43
  485.7 0.0 copy-done.1
  485.7 1.0 copy.44
  486.7 0.0 copy-done
  486.7 1.0 copy.45
  (5 shorter events, 0.0 us)
Async XLA Ops:
  454.5 30.6 %copy-start.2 = (f32[1,512]{1,0:T(1,128)}, f32[1,512]{1,0:T(1,128)S(1)}, u32[]{:S(2)}) copy-start(f32[1,512]{1,0:T(1,128)S(1)} %get-tuple-element.34) | copy-start | bytes 6148
  455.1 30.6 %copy-start.1 = (bf16[256,2048]{1,0:T(8,128)(2,1)S(1)}, bf16[256,2048]{1,0:T(8,128)(2,1)}, u32[]{:S(2)}) copy-start(bf16[256,2048]{1,0:T(8,128)(2,1)} %get-tuple-element.22) | copy-start | bytes 3145732
  455.1 31.6 %copy-start = (bf16[256,2048]{1,0:T(8,128)(2,1)S(1)}, bf16[256,2048]{1,0:T(8,128)(2,1)}, u32[]{:S(2)}) copy-start(bf16[256,2048]{1,0:T(8,128)(2,1)} %get-tuple-element.23) | copy-start | bytes 3145732
